TPU v7x, 512 devices: a whole 4x8x8 slice. The times are simulated.
512 devices in a mesh: dp: 32 (over y, x_hi, core), expert: 16 (over z, x_lo).
Axes of the slice: x: 4 (x_hi: 2, x_lo: 2; x = x_hi * 2 + x_lo), y: 8, z: 8, core: 2. Of those that a mesh axis runs over, the one named last changes fastest.
Arguments:
- tokens: bfloat16 [65536, 1280], P(('dp', 'expert')), may hold values from -24 to 24
- out_grad: bfloat16 [65536, 1280], P(('dp', 'expert')), may hold values from -9 to 9
- routes: int32 [65536, 8], P(('dp', 'expert')), may hold values from 0 to 127, as said below
- gate_values: bfloat16 [65536, 8], P(('dp', 'expert')), may hold values from 0.029907227 to 0.3984375
- w_gate: bfloat16 [16, 1280, 512], P('expert', 'dp'), may hold values from -0.15625 to 0.15625
- w_up: bfloat16 [16, 1280, 512], P('expert', 'dp'), may hold values from -0.15625 to 0.15625
- w_down: bfloat16 [16, 512, 1280], P('expert', 'dp'), may hold values from -0.25 to 0.25
Outputs:
- token_grad: bfloat16 [65536, 1280], P(('dp', 'expert'))
- gate_grad: bfloat16 [65536, 8], P(('dp', 'expert'))
- w_gate_grad: bfloat16 [16, 1280, 512], P('expert', 'dp')
- w_up_grad: bfloat16 [16, 1280, 512], P('expert', 'dp')
- w_down_grad: bfloat16 [16, 512, 1280], P('expert', 'dp')
Inputs may be any that keep to these rules, and one draw needn't show every extreme that they name: `routes`: each row names 8 different experts. Among the 128 rows of one device (aligned blocks), no expert whose number is a multiple of 8 is named by more than 16 rows, and each row names at most two such experts.
All inputs are finite; a program needn't handle non-finite values.
Results may differ from a plain program's by a relative error of at most 0.02.
Values may be sent and summed in bfloat16 or wider, within the bound.
A program may use at most 64 MiB of HBM per device.

v0:
```python
import jax
import jax.numpy as jnp
from jax import lax
from jax.sharding import PartitionSpec as P

EXP_DEV = 8


CONTRACT_ROWS = (((0,), (0,)), ((), ()))
CONTRACT_LAST = (((1,), (1,)), ((), ()))


def activation_parts(gate_pre, up_pre):
    squash = jax.nn.sigmoid(gate_pre)
    activation = (gate_pre * squash * up_pre).astype(jnp.bfloat16)
    return (squash, activation)


def hidden_grads(act_grad, gate_pre, up_pre, squash):
    pre_gate = (act_grad * up_pre * squash * (1.0 + gate_pre * (1.0 - squash))).astype(jnp.bfloat16)
    pre_up = (act_grad * gate_pre * squash).astype(jnp.bfloat16)
    return (pre_gate, pre_up)


def body(tokens, out_grad, routes, gate_values, w_gate, w_up, w_down):
    expert_count = lax.axis_size("expert")
    tok_dev = tokens.shape[0]
    features = tokens.shape[1]
    hidden = w_gate.shape[2]
    capacity = 2 * tok_dev // expert_count
    slot_total = expert_count * capacity
    flight_ids = jnp.arange(expert_count, dtype=jnp.int32) * EXP_DEV
    matched = routes[:, :, None] == flight_ids[None, None, :]
    chosen = jnp.any(matched, axis=1)
    gate_tok = jnp.sum(jnp.where(matched, gate_values[:, :, None].astype(jnp.float32), 0.0), axis=1)
    slot_rank = jnp.cumsum(chosen.astype(jnp.int32), axis=0) - 1
    placing = chosen[:, :, None] & (
        slot_rank[:, :, None] == jnp.arange(capacity, dtype=jnp.int32)[None, None, :]
    )
    place_mask = placing.astype(jnp.bfloat16)
    place_wide = placing.astype(jnp.float32)
    send_inputs = jnp.einsum(
        "tfc,td->fcd", place_mask, tokens, preferred_element_type=jnp.float32
    ).astype(jnp.bfloat16)
    send_grads = jnp.einsum(
        "tfc,td->fcd", place_mask, out_grad, preferred_element_type=jnp.float32
    ).astype(jnp.bfloat16)
    send_gates = jnp.einsum("tfc,tf->fc", place_wide, gate_tok).astype(jnp.bfloat16)
    got_inputs, got_grads, got_gates = (
        lax.all_to_all(send_inputs, "expert", split_axis=0, concat_axis=0, tiled=True),
        lax.all_to_all(send_grads, "expert", split_axis=0, concat_axis=0, tiled=True),
        lax.all_to_all(send_gates, "expert", split_axis=0, concat_axis=0, tiled=True),
    )
    inputs = got_inputs.reshape(slot_total, features)
    grad_rows = got_grads.reshape(slot_total, features)
    gate_col = got_gates.reshape(slot_total, 1).astype(jnp.float32)
    grad_wide = grad_rows.astype(jnp.float32)
    scaled_grad = (gate_col * grad_wide).astype(jnp.bfloat16)
    full_gate, full_up, full_down = (
        lax.all_gather(w_gate, "dp", axis=1, tiled=True),
        lax.all_gather(w_up, "dp", axis=1, tiled=True),
        lax.all_gather(w_down, "dp", axis=1, tiled=True),
    )
    full_gate = full_gate[0]
    full_up = full_up[0]
    full_down = full_down[0]
    gate_pre = jnp.dot(inputs, full_gate, preferred_element_type=jnp.float32)
    up_pre = jnp.dot(inputs, full_up, preferred_element_type=jnp.float32)
    squash, activation = activation_parts(gate_pre, up_pre)
    expert_out = jnp.dot(activation, full_down, preferred_element_type=jnp.float32)
    act_grad = lax.dot_general(
        scaled_grad, full_down, CONTRACT_LAST, preferred_element_type=jnp.float32
    )
    pre_gate, pre_up = hidden_grads(act_grad, gate_pre, up_pre, squash)
    input_grad = (
        lax.dot_general(pre_gate, full_gate, CONTRACT_LAST, preferred_element_type=jnp.float32)
        + lax.dot_general(pre_up, full_up, CONTRACT_LAST, preferred_element_type=jnp.float32)
    ).astype(jnp.bfloat16)
    gate_term = jnp.sum(grad_wide * expert_out, axis=1).astype(jnp.bfloat16)
    stacked_hidden = jnp.concatenate([pre_gate, pre_up], axis=1)
    back_inputs = lax.all_to_all(
        input_grad.reshape(expert_count, capacity, features),
        "expert",
        split_axis=0,
        concat_axis=0,
        tiled=True,
    )
    back_gates = lax.all_to_all(
        gate_term.reshape(expert_count, capacity), "expert", split_axis=0, concat_axis=0, tiled=True
    )
    token_grad = jnp.einsum(
        "tfc,fcd->td", place_mask, back_inputs, preferred_element_type=jnp.float32
    ).astype(jnp.bfloat16)
    gate_by = jnp.einsum("tfc,fc->tf", place_wide, back_gates.astype(jnp.float32))
    gate_grad = jnp.einsum("tkf,tf->tk", matched.astype(jnp.float32), gate_by).astype(jnp.bfloat16)
    token_grad, gate_grad = (token_grad, gate_grad)
    summed = lax.psum_scatter(
        lax.dot_general(
            inputs, stacked_hidden, CONTRACT_ROWS, preferred_element_type=jnp.float32
        ).astype(jnp.bfloat16),
        "dp",
        scatter_dimension=0,
        tiled=True,
    ).astype(jnp.float32)
    down_sum = lax.psum_scatter(
        lax.dot_general(
            activation, scaled_grad, CONTRACT_ROWS, preferred_element_type=jnp.float32
        ).astype(jnp.bfloat16),
        "dp",
        scatter_dimension=0,
        tiled=True,
    ).astype(jnp.float32)
    summed, down_sum = (summed, down_sum)
    w_gate_grad = summed[:, :hidden].astype(jnp.bfloat16)[None]
    w_up_grad = summed[:, hidden:].astype(jnp.bfloat16)[None]
    w_down_grad = down_sum.astype(jnp.bfloat16)[None]
    return (token_grad, gate_grad, w_gate_grad, w_up_grad, w_down_grad)


def solution(mesh):
    placed = (
        P(("dp", "expert"), None),
        P(("dp", "expert"), None),
        P(("dp", "expert"), None),
        P(("dp", "expert"), None),
        P("expert", "dp", None),
        P("expert", "dp", None),
        P("expert", "dp", None),
    )
    return jax.shard_map(
        body,
        mesh=mesh,
        in_specs=placed,
        out_specs=(
            P(("dp", "expert"), None),
            P(("dp", "expert"), None),
            P("expert", "dp", None),
            P("expert", "dp", None),
            P("expert", "dp", None),
        ),
        check_vma=False,
    )
```

profile of v0, /device:TPU:1, one launch (start us, length us, event | category | flops | bytes accessed | tf_op | source)
XLA Modules:
  0.0 529.1 jit_solution(17290852084142814231)
XLA Ops:
  8.0 0.7 all-gather.4.cloned.1.call-update
  8.7 0.7 convert_element_type.102
  9.4 0.8 compare_reduce_fusion
  10.5 0.8 fusion.23
  12.1 11.9 %all-to-all-start = ((bf16[16,1,16]{2,1,0:T(2,128)(2,1)}), bf16[16,1,16]{2,1,0:T(2,128)(2,1)S(1)}, u32[]{:S(2)}, u32[]{:S(2)}) async-start(bf16[16,1,16]{2,1,0:T(2,128)(2,1)} %copy.45), calls=%async_computation | async-start | bytes 16384 | tf_op jit(solution)/shard_map/all_to_all | solution.py:52
  24.0 1.2 convolution_convert_fusion.3
  25.2 6.1 %all-to-all-done = bf16[16,1,16]{2,1,0:T(2,128)(2,1)S(1)} async-done(((bf16[16,1,16]{2,1,0:T(2,128)(2,1)}), bf16[16,1,16]{2,1,0:T(2,128)(2,1)S(1)}, u32[]{:S(2)}, u32[]{:S(2)}) %all-to-all-start) | async-done | bytes 544 | tf_op jit(solution)/shard_map/all_to_all | solution.py:52
  31.3 3.6 all-to-all-start.1
  35.6 1.2 convolution_convert_fusion.2
  36.8 15.1 %all-to-all-done.1 = bf16[16,16,1280]{2,1,0:T(8,128)(2,1)S(1)} async-done(((bf16[16,16,1280]{2,1,0:T(8,128)(2,1)}), bf16[16,16,1280]{2,1,0:T(8,128)(2,1)S(1)}, u32[]{:S(2)}, u32[]{:S(2)}) %all-to-all-start.1) | async-done | bytes 655392 | tf_op jit(solution)/shard_map/all_to_all | solution.py:51
  51.9 5.3 %all-to-all-start.2 = ((bf16[16,16,1280]{2,1,0:T(8,128)(2,1)}), bf16[16,16,1280]{2,1,0:T(8,128)(2,1)S(1)}, u32[]{:S(2)}, u32[]{:S(2)}) async-start(bf16[16,16,1280]{2,1,0:T(8,128)(2,1)} %convolution_convert_fusion.2), calls=%async_computation.2 | async-start | bytes 1310720 | tf_op jit(solution)/shard_map/all_to_all | solution.py:50
  57.5 16.9 %all-to-all-done.2 = bf16[16,16,1280]{2,1,0:T(8,128)(2,1)S(1)} async-done(((bf16[16,16,1280]{2,1,0:T(8,128)(2,1)}), bf16[16,16,1280]{2,1,0:T(8,128)(2,1)S(1)}, u32[]{:S(2)}, u32[]{:S(2)}) %all-to-all-start.2) | async-done | bytes 655392 | tf_op jit(solution)/shard_map/all_to_all | solution.py:50
  74.5 28.6 %all-gather.8.cloned.1.call-done = bf16[1,1280,512]{2,1,0:T(8,128)(2,1)} async-done(((bf16[1,40,512]{2,1,0:T(8,128)(2,1)}), bf16[1,1280,512]{2,1,0:T(8,128)(2,1)}) %all-gather.8.cloned.1.call-update) | async-done | bytes 1310736 | tf_op jit(solution)/shard_map/all_gather | solution.py:60
  103.1 1.8 fusion.5
  104.9 79.9 %all-gather.4.cloned.1.call-done = bf16[1,512,1280]{2,1,0:T(8,128)(2,1)} async-done(((bf16[1,16,1280]{2,1,0:T(8,128)(2,1)}), bf16[1,512,1280]{2,1,0:T(8,128)(2,1)}) %all-gather.4.cloned.1.call-update) | async-done | bytes 1310736 | tf_op jit(solution)/shard_map/all_gather | solution.py:62
  184.8 2.6 fusion.11
  187.4 81.2 %all-gather.6.cloned.1.call-done = bf16[1,1280,512]{2,1,0:T(8,128)(2,1)} async-done(((bf16[1,40,512]{2,1,0:T(8,128)(2,1)}), bf16[1,1280,512]{2,1,0:T(8,128)(2,1)}) %all-gather.6.cloned.1.call-update) | async-done | bytes 1310736 | tf_op jit(solution)/shard_map/all_gather | solution.py:61
  268.6 2.1 multiply_convert_fusion.1
  270.7 2.4 convolution_convert_fusion
  273.5 1.9 fusion.13
  275.4 0.7 convert_element_type.129
  276.1 7.2 %all-to-all-start.4 = ((bf16[16,1,16]{2,1,0:T(2,128)(2,1)}), bf16[16,1,16]{2,1,0:T(2,128)(2,1)S(1)}, u32[]{:S(2)}, u32[]{:S(2)}) async-start(bf16[16,1,16]{2,1,0:T(2,128)(2,1)} %convert_element_type.129), calls=%async_computation.4 | async-start | bytes 16384 | tf_op jit(solution)/shard_map/all_to_all | solution.py:88
  283.3 2.7 convolution_convert_fusion.1
  286.6 0.8 copy-done.2
  287.4 1.4 fusion
  288.8 1.7 all-to-all-done.4
  290.6 6.0 %all-to-all-start.3 = ((bf16[16,16,1280]{2,1,0:T(8,128)(2,1)}), bf16[16,16,1280]{2,1,0:T(8,128)(2,1)S(1)}, u32[]{:S(2)}, u32[]{:S(2)}) async-start(bf16[16,16,1280]{2,1,0:T(8,128)(2,1)} %bitcast.14), calls=%async_computation.3 | async-start | bytes 1310720 | tf_op jit(solution)/shard_map/all_to_all | solution.py:81
  297.3 17.3 %all-to-all-done.3 = bf16[16,16,1280]{2,1,0:T(8,128)(2,1)S(1)} async-done(((bf16[16,16,1280]{2,1,0:T(8,128)(2,1)}), bf16[16,16,1280]{2,1,0:T(8,128)(2,1)S(1)}, u32[]{:S(2)}, u32[]{:S(2)}) %all-to-all-start.3) | async-done | bytes 655392 | tf_op jit(solution)/shard_map/all_to_all | solution.py:81
  314.6 1.1 fusion.1
  315.7 78.2 %reduce-scatter.3.cloned.1.call-done = bf16[40,1024]{1,0:T(8,128)(2,1)} async-done(((bf16[1280,1024]{1,0:T(8,128)(2,1)}), bf16[40,1024]{1,0:T(8,128)(2,1)}) %reduce-scatter.3.cloned.1.call-update) | async-done | bytes 81936 | tf_op jit(solution)/shard_map/reduce_scatter | solution.py:97
  393.9 1.4 slice_bitcast_fusion
  395.3 127.2 %reduce-scatter.5.cloned.1.call-done = bf16[16,1280]{1,0:T(8,128)(2,1)} async-done(((bf16[512,1280]{1,0:T(8,128)(2,1)}), bf16[16,1280]{1,0:T(8,128)(2,1)}) %reduce-scatter.5.cloned.1.call-update) | async-done | bytes 40976 | tf_op jit(solution)/shard_map/reduce_scatter | solution.py:105
  (38 shorter events, 4.6 us)
Async XLA Ops:
  7.2 16.9 %copy-start = (bf16[128,1280]{1,0:T(8,128)(2,1)S(1)}, bf16[128,1280]{1,0:T(8,128)(2,1)}, u32[]{:S(2)}) copy-start(bf16[128,1280]{1,0:T(8,128)(2,1)} %param.8) | copy-start | bytes 983044
  7.2 95.9 %all-gather.8.cloned.1.call-start = ((), (), s32[]{:S(2)}) async-start(), calls=%async_computation.9 | async-start | bytes 1351680 | tf_op jit(solution)/shard_map/all_gather | solution.py:60
  7.9 176.9 %all-gather.4.cloned.1.call-start = ((), (), s32[]{:S(2)}) async-start(), calls=%async_computation.7 | async-start | bytes 1351680 | tf_op jit(solution)/shard_map/all_gather | solution.py:62
  10.5 25.2 %copy-start.3 = (bf16[128,1280]{1,0:T(8,128)(2,1)S(1)}, bf16[128,1280]{1,0:T(8,128)(2,1)}, u32[]{:S(2)}) copy-start(bf16[128,1280]{1,0:T(8,128)(2,1)} %param.7) | copy-start | bytes 983044
  12.1 19.2 %all-to-all-start = ((bf16[16,1,16]{2,1,0:T(2,128)(2,1)}), bf16[16,1,16]{2,1,0:T(2,128)(2,1)S(1)}, u32[]{:S(2)}, u32[]{:S(2)}) async-start(bf16[16,1,16]{2,1,0:T(2,128)(2,1)} %copy.45), calls=%async_computation | async-start | bytes 16384 | tf_op jit(solution)/shard_map/all_to_all | solution.py:52
  31.3 20.6 %all-to-all-start.1 = ((bf16[16,16,1280]{2,1,0:T(8,128)(2,1)}), bf16[16,16,1280]{2,1,0:T(8,128)(2,1)S(1)}, u32[]{:S(2)}, u32[]{:S(2)}) async-start(bf16[16,16,1280]{2,1,0:T(8,128)(2,1)} %convolution_convert_fusion.3), calls=%async_computation.1 | async-start | bytes 1310720 | tf_op jit(solution)/shard_map/all_to_all | solution.py:51
  34.9 233.7 %all-gather.6.cloned.1.call-start = ((), (), s32[]{:S(2)}) async-start(), calls=%async_computation.8 | async-start | bytes 1351680 | tf_op jit(solution)/shard_map/all_gather | solution.py:61
  51.9 22.5 %all-to-all-start.2 = ((bf16[16,16,1280]{2,1,0:T(8,128)(2,1)}), bf16[16,16,1280]{2,1,0:T(8,128)(2,1)S(1)}, u32[]{:S(2)}, u32[]{:S(2)}) async-start(bf16[16,16,1280]{2,1,0:T(8,128)(2,1)} %convolution_convert_fusion.2), calls=%async_computation.2 | async-start | bytes 1310720 | tf_op jit(solution)/shard_map/all_to_all | solution.py:50
  57.3 336.6 %reduce-scatter.3.cloned.1.call-start = ((), (), s32[]{:S(2)}) async-start(), calls=%async_computation.10 | async-start | bytes 2703360 | tf_op jit(solution)/shard_map/reduce_scatter | solution.py:97
  270.7 2.7 copy-start.4
  276.1 14.5 %all-to-all-start.4 = ((bf16[16,1,16]{2,1,0:T(2,128)(2,1)}), bf16[16,1,16]{2,1,0:T(2,128)(2,1)S(1)}, u32[]{:S(2)}, u32[]{:S(2)}) async-start(bf16[16,1,16]{2,1,0:T(2,128)(2,1)} %convert_element_type.129), calls=%async_computation.4 | async-start | bytes 16384 | tf_op jit(solution)/shard_map/all_to_all | solution.py:88
  283.3 2.8 copy-start.1
  283.3 239.3 %reduce-scatter.5.cloned.1.call-start = ((), (), s32[]{:S(2)}) async-start(), calls=%async_computation.11 | async-start | bytes 1351680 | tf_op jit(solution)/shard_map/reduce_scatter | solution.py:105
  286.1 1.4 copy-start.2
  288.8 7.8 %copy-start.5 = (s32[128,8]{0,1:T(8,128)S(1)}, s32[128,8]{0,1:T(8,128)}, u32[]{:S(2)}) copy-start(s32[128,8]{0,1:T(8,128)} %param.9) | copy-start | bytes 12292
  290.6 24.1 %all-to-all-start.3 = ((bf16[16,16,1280]{2,1,0:T(8,128)(2,1)}), bf16[16,16,1280]{2,1,0:T(8,128)(2,1)S(1)}, u32[]{:S(2)}, u32[]{:S(2)}) async-start(bf16[16,16,1280]{2,1,0:T(8,128)(2,1)} %bitcast.14), calls=%async_computation.3 | async-start | bytes 1310720 | tf_op jit(solution)/shard_map/all_to_all | solution.py:81
Sparse Core Ops, SparseCore 0:
  11.4 91.6 all-gather.7
  106.5 78.3 all-gather.3
  188.2 80.4 all-gather.5
  273.3 120.5 reduce-scatter.2
  399.7 122.8 reduce-scatter.4
where the time goes:
time: 534 us; the launch traced here: 529 us
  waiting for transfers between devices  454 us (85%)
  starting transfers between devices  34.2 us (6%)
  matrix products  19.2 us (4%)
  between operations  14 us (3%)
    reduce_scatter x1, waiting for transfers between devices, body(): lax.psum_scatter(lax.dot_general(activation, scaled_grad, CONTRACT_ROWS,...  127 us
    all_gather x1, waiting for transfers between devices, body(): lax.all_gather(w_up, 'dp', axis=1, tiled=True)  81.2 us
    all_gather x1, waiting for transfers between devices, body(): lax.all_gather(w_down, 'dp', axis=1, tiled=True)  79.9 us
    reduce_scatter x1, waiting for transfers between devices, body(): lax.psum_scatter(lax.dot_general(inputs, stacked_hidden, CONTRACT_ROWS, p...  78.2 us
    all_gather x1, waiting for transfers between devices, body(): lax.all_gather(w_gate, 'dp', axis=1, tiled=True)  28.6 us
    all_to_all x1, waiting for transfers between devices, body(): lax.all_to_all(input_grad.reshape(expert_count, capacity, features), 'exp...  17.3 us
    all_to_all x1, waiting for transfers between devices, body(): lax.all_to_all(send_inputs, 'expert', split_axis=0, concat_axis=0, tiled=...  16.9 us
    all_to_all x1, waiting for transfers between devices, body(): lax.all_to_all(send_grads, 'expert', split_axis=0, concat_axis=0, tiled=T...  15.1 us
  transfers between devices with their start and end apart: 10, of which 10 were waited for; matrix products, arithmetic and copies ran while one was open for 4% of the time, Pallas kernels for 0%

commit v1 on v0

v1 whole, which is shorter than its diff:
```python
import jax
import jax.numpy as jnp
from jax import lax
from jax.experimental import pallas as pl
from jax.experimental.pallas import tpu as pltpu
from jax.sharding import PartitionSpec as P

EXP_DEV = 8
MESH = pl.DeviceIdType.MESH
BF = jnp.bfloat16
F32 = jnp.float32
ROWS = (((0,), (0,)), ((), ()))
LAST = (((1,), (1,)), ((), ()))

N_E = 16
N_Y = 8
TOK = 128
CAP = 16
SLOTS = N_E * CAP
D = 1280
FF = 512
WIDE = D + 128
UNIT = 80
HALF = 40
DOWN = 16
STEPS = ((4, 3), (3, 4))


def kernel(
    tokens, grads, routes, gates, wg, wu, wd,
    tok_out, gate_out, wg_out, wu_out, wd_out,
    place_ref, send_x, send_g, got_x, got_g, ret, back,
    w_own, w_sib, w2, wdn,
    h_ref, u_ref, g_ref, a_ref, dhu_ref, e_ref,
    d2, dd, s2, sd, snd2, sndd, rec2, recd, xs2, xsd, xr2, xrd, cs, cr,
    sx, rx, sg, rg, sr, rr, s0, r0, sxw, rxw, sag, rag, ssw, rsw,
    ssd, rsd, srs, rrs, sxr, rxr, scr, rcr,
):
    dp = lax.axis_index("dp")
    ex = lax.axis_index("expert")
    core = lax.rem(dp, 2)
    xh = lax.rem(lax.div(dp, 2), 2)
    y = lax.div(dp, 4)
    other = 1 - core
    low = lax.rem(dp, 4)
    sibling = (dp + 1 - 2 * core, ex)
    partner = (dp + 2 - 4 * xh, ex)
    ups = (
        (lax.rem(y + 1, N_Y) * 4 + low, ex),
        (lax.rem(y + N_Y - 1, N_Y) * 4 + low, ex),
    )

    def wrap(offset):
        return lax.rem(y + (offset + 2 * N_Y), N_Y)

    def peer(k):
        return lax.rem(ex + (k + N_E), N_E)

    def remote(src, dst, send, recv, to):
        return pltpu.make_async_remote_copy(
            src_ref=src, dst_ref=dst, send_sem=send, recv_sem=recv,
            device_id=to, device_id_type=MESH,
        )

    started = []

    def go(*args):
        copy = remote(*args)
        copy.start()
        started.append(copy)
        return copy

    barrier = pltpu.get_barrier_semaphore()
    for to in (sibling, partner) + ups:
        pl.semaphore_signal(barrier, inc=1, device_id=to, device_id_type=MESH)
    for k in range(1, N_E):
        pl.semaphore_signal(barrier, inc=1, device_id=(dp, peer(k)), device_id_type=MESH)

    lane = lax.broadcasted_iota(jnp.int32, (TOK, SLOTS), 1)
    expert_id = lax.div(lane, CAP) * EXP_DEV
    slot_id = lax.rem(lane, CAP)
    route = routes[...]
    gate_wide = gates[...].astype(F32)
    chosen = jnp.zeros((TOK, SLOTS), F32)
    gate_tok = jnp.zeros((TOK, SLOTS), F32)
    for k in range(8):
        match = route[:, k : k + 1] == expert_id
        chosen = jnp.where(match, 1.0, chosen)
        gate_tok = jnp.where(match, gate_wide[:, k : k + 1], gate_tok)
    before = (
        lax.broadcasted_iota(jnp.int32, (TOK, TOK), 0)
        > lax.broadcasted_iota(jnp.int32, (TOK, TOK), 1)
    )
    before = jnp.where(before, 1.0, 0.0).astype(BF)
    rank = jnp.dot(before, chosen.astype(BF), preferred_element_type=F32)
    placing = jnp.where(rank == slot_id.astype(F32), chosen, 0.0)
    gate_slot = (placing * gate_tok).astype(BF)
    placing = placing.astype(BF)
    place_ref[...] = placing
    w_own[0] = wg[...]
    w_own[1] = wu[...]
    wdn[y, xh, core] = wd[...]
    send_x[...] = (
        lax.dot_general(placing, tokens[...], ROWS, preferred_element_type=F32)
        .astype(BF).reshape(N_E, CAP, D)
    )

    pl.semaphore_wait(barrier, 4 + N_E - 1)

    first = go(w_own.at[other], w_sib, s0, r0, sibling)
    part_d = go(wdn.at[y, xh, core], wdn.at[y, xh, core], sxw.at[1], rxw.at[1], partner)
    row_x = [
        go(send_x.at[peer(k)], got_x.at[ex], sx.at[k], rx.at[k], (dp, peer(k)))
        for k in range(1, N_E)
    ]
    got_x[ex] = send_x[ex]

    first.wait_recv()
    mine = w_own[core].astype(F32)
    theirs = w_sib[...].astype(F32)
    is_first = core == 0
    w2[core, 2 * y + xh] = jnp.concatenate(
        [jnp.where(is_first, mine, theirs), jnp.where(is_first, theirs, mine)], axis=0
    ).astype(BF)
    part_2 = go(
        w2.at[core, 2 * y + xh], w2.at[core, 2 * y + xh], sxw.at[0], rxw.at[0], partner
    )

    send_g[:, :, :D] = (
        lax.dot_general(placing, grads[...], ROWS, preferred_element_type=F32)
        .astype(BF).reshape(N_E, CAP, D)
    )
    send_g[:, :, D:] = (
        lax.dot_general(gate_slot, jnp.ones((TOK, 128), BF), ROWS, preferred_element_type=F32)
        .astype(BF).reshape(N_E, CAP, 128)
    )
    got_g[ex] = send_g[ex]

    def block(piece, at):
        if piece == 0:
            return w2.at[core, pl.ds(2 * at, 2)]
        return wdn.at[at, :, core]

    def ring_send(piece, way, step):
        at = block(piece, wrap(-step if way == 0 else step))
        return go(at, at, sag.at[piece, way, step], rag.at[piece, way, step], ups[way])

    def to_sibling(piece, at, index):
        at = block(piece, at)
        return go(at, at, ssw.at[piece, index], rsw.at[piece, index], sibling)

    part_d.wait_recv()
    part_2.wait_recv()
    ring = {}
    shared = []
    for piece in range(2):
        for way in range(2):
            ring[piece, way] = ring_send(piece, way, 0)
    row_g = [
        go(send_g.at[peer(k)], got_g.at[ex], sg.at[k], rg.at[k], (dp, peer(k)))
        for k in range(1, N_E)
    ]
    for piece in range(2):
        shared.append(to_sibling(piece, y, 0))
    for step in range(4):
        for piece in range(2):
            for way in range(2):
                if step < STEPS[piece][way]:
                    ring[piece, way].wait_recv()
                    if step + 1 < STEPS[piece][way]:
                        ring[piece, way] = ring_send(piece, way, step + 1)
                    offset = -1 - step if way == 0 else 1 + step
                    index = 1 + step if way == 0 else 1 + STEPS[piece][0] + step
                    shared.append(to_sibling(piece, wrap(offset), index))
    for copy in shared:
        copy.wait_recv()
    for copy in row_x:
        copy.wait_recv()

    rows = got_x[...].reshape(SLOTS, D)
    h_ref[...] = jnp.dot(rows, w2[0].reshape(D, FF), preferred_element_type=F32)
    u_ref[...] = jnp.dot(rows, w2[1].reshape(D, FF), preferred_element_type=F32)
    for copy in row_g:
        copy.wait_recv()
    g_ref[...] = lax.dot_general(
        got_g[:, :, :D].reshape(SLOTS, D), wdn[...].reshape(FF, D), LAST,
        preferred_element_type=F32,
    )

    def elementwise(i, carry):
        at = pl.ds(pl.multiple_of(i * CAP, CAP), CAP)
        h, u, g = h_ref[at], u_ref[at], g_ref[at]
        row = got_g[i]
        gate = row[:, D : D + 1].astype(F32)
        s = jax.nn.sigmoid(h)
        a = (h * s * u).astype(BF)
        a_ref[at] = a
        term = jnp.sum(a.astype(F32) * g, axis=1, keepdims=True)
        ret[i, :, D:] = jnp.broadcast_to(term, (CAP, 128)).astype(BF)
        g = gate * g
        dhu_ref[at, :FF] = (g * u * s * (1.0 + h * (1.0 - s))).astype(BF)
        dhu_ref[at, FF:] = (g * h * s).astype(BF)
        e_ref[at] = (gate * row[:, :D].astype(F32)).astype(BF)
        return carry

    lax.fori_loop(0, N_E, elementwise, 0)

    for m in range(2):
        d2[m] = (
            lax.dot_general(
                rows, dhu_ref[:, m * FF : (m + 1) * FF], ROWS, preferred_element_type=F32
            ).astype(BF).reshape(2 * N_Y, UNIT, FF)
        )
    dd[...] = (
        lax.dot_general(a_ref[...], e_ref[...], ROWS, preferred_element_type=F32)
        .astype(BF).reshape(N_Y, 2, 2, DOWN, D)
    )

    def partial(piece, which, at):
        if piece == 0:
            return d2.at[which, pl.ds(2 * at, 2)]
        return dd.at[at, :, which]

    def paired(piece, at):
        return s2.at[pl.ds(2 * at, 2)] if piece == 0 else sd.at[at]

    given = {}

    def give(piece, offset):
        at = wrap(offset)
        index = offset % N_Y
        given[piece, index] = go(
            partial(piece, other, at), paired(piece, at),
            ssd.at[piece, index], rsd.at[piece, index], sibling,
        )

    for step in range(4):
        for piece in range(2):
            for way in range(2):
                left = STEPS[piece][way] - step
                if left > 0:
                    give(piece, left if way == 0 else -left)
    for piece in range(2):
        give(piece, 0)

    ret[:, :, :D] = (
        lax.dot_general(dhu_ref[:, :FF], w2[0].reshape(D, FF), LAST, preferred_element_type=F32)
        + lax.dot_general(dhu_ref[:, FF:], w2[1].reshape(D, FF), LAST, preferred_element_type=F32)
    ).astype(BF).reshape(N_E, CAP, D)

    def chip_sum(piece, offset):
        given[piece, offset % N_Y].wait_recv()
        at = wrap(offset)
        return partial(piece, core, at)[...].astype(F32) + paired(piece, at)[...].astype(F32)

    out_buf, in_buf = (snd2, sndd), (rec2, recd)
    going = {}

    def reduce_step(piece, way, step):
        left = STEPS[piece][way] - step
        total = chip_sum(piece, left if way == 0 else -left)
        if step > 0:
            going[piece, way].wait_recv()
            total = total + in_buf[piece][way, step - 1].astype(F32)
        out_buf[piece][way, step] = total.astype(BF)
        going[piece, way] = go(
            out_buf[piece].at[way, step], in_buf[piece].at[way, step],
            srs.at[piece, way, step], rrs.at[piece, way, step], ups[way],
        )

    back_rows = []
    for step in range(4):
        for piece in range(2):
            for way in range(2):
                if step < STEPS[piece][way]:
                    reduce_step(piece, way, step)
        if step == 0:
            back_rows = [
                go(ret.at[peer(k)], back.at[ex], sr.at[k], rr.at[k], (dp, peer(k)))
                for k in range(1, N_E)
            ]
            back[ex] = ret[ex]

    kept = []
    crossing = []
    x_out, x_in = (xs2, xsd), (xr2, xrd)
    for piece in range(2):
        total = chip_sum(piece, 0)
        for way in range(2):
            going[piece, way].wait_recv()
            total = total + in_buf[piece][way, STEPS[piece][way] - 1].astype(F32)
        here = xh == 0
        x_out[piece][...] = jnp.where(here, total[1], total[0]).astype(BF)
        kept.append(jnp.where(here, total[0], total[1]))
        crossing.append(
            go(x_out[piece], x_in[piece], sxr.at[piece], rxr.at[piece], partner)
        )

    for piece in range(2):
        crossing[piece].wait_recv()
        kept[piece] = kept[piece] + x_in[piece][...].astype(F32)
    top, bottom = kept[0][:HALF], kept[0][HALF:]
    cs[...] = jnp.where(is_first, bottom, top).astype(BF)
    last = go(cs, cr, scr, rcr, sibling)
    own_half = jnp.where(is_first, top, bottom)
    wd_out[...] = kept[1].astype(BF)

    for copy in back_rows:
        copy.wait_recv()
    place = place_ref[...]
    tok_out[...] = jnp.dot(
        place, back[:, :, :D].reshape(SLOTS, D), preferred_element_type=F32
    ).astype(BF)
    terms = back[:, :, D:].reshape(SLOTS, 128)
    pick = lax.div(lax.broadcasted_iota(jnp.int32, (SLOTS, 128), 0), CAP)
    pick = pick == lax.broadcasted_iota(jnp.int32, (SLOTS, 128), 1)
    terms = jnp.where(pick, terms.astype(F32), 0.0).astype(BF)
    by_expert = jnp.dot(place, terms, preferred_element_type=F32)
    ids = lax.broadcasted_iota(jnp.int32, (TOK, 128), 1) * EXP_DEV
    column = lax.broadcasted_iota(jnp.int32, (TOK, 8), 1)
    result = jnp.zeros((TOK, 8), F32)
    route = routes[...]
    for k in range(8):
        value = jnp.sum(
            jnp.where(route[:, k : k + 1] == ids, by_expert, 0.0), axis=1, keepdims=True
        )
        result = jnp.where(column == k, value, result)
    gate_out[...] = result.astype(BF)

    last.wait_recv()
    arrived = cr[...].astype(F32)
    wg_out[...] = jnp.where(is_first, own_half, arrived).astype(BF)
    wu_out[...] = jnp.where(is_first, arrived, own_half).astype(BF)
    for copy in started:
        copy.wait_send()


def body(tokens, out_grad, routes, gate_values, w_gate, w_up, w_down):
    vmem = pl.BlockSpec(memory_space=pltpu.VMEM)
    dma = pltpu.SemaphoreType.DMA
    shape = jax.ShapeDtypeStruct
    scratch = [
        pltpu.VMEM((TOK, SLOTS), BF),
        pltpu.VMEM((N_E, CAP, D), BF),
        pltpu.VMEM((N_E, CAP, WIDE), BF),
        pltpu.VMEM((N_E, CAP, D), BF),
        pltpu.VMEM((N_E, CAP, WIDE), BF),
        pltpu.VMEM((N_E, CAP, WIDE), BF),
        pltpu.VMEM((N_E, CAP, WIDE), BF),
        pltpu.VMEM((2, HALF, FF), BF),
        pltpu.VMEM((HALF, FF), BF),
        pltpu.VMEM((2, 2 * N_Y, UNIT, FF), BF),
        pltpu.VMEM((N_Y, 2, 2, DOWN, D), BF),
        pltpu.VMEM((SLOTS, FF), F32),
        pltpu.VMEM((SLOTS, FF), F32),
        pltpu.VMEM((SLOTS, FF), F32),
        pltpu.VMEM((SLOTS, FF), BF),
        pltpu.VMEM((SLOTS, 2 * FF), BF),
        pltpu.VMEM((SLOTS, D), BF),
        pltpu.VMEM((2, 2 * N_Y, UNIT, FF), BF),
        pltpu.VMEM((N_Y, 2, 2, DOWN, D), BF),
        pltpu.VMEM((2 * N_Y, UNIT, FF), BF),
        pltpu.VMEM((N_Y, 2, DOWN, D), BF),
        pltpu.VMEM((2, 4, 2, UNIT, FF), BF),
        pltpu.VMEM((2, 4, 2, DOWN, D), BF),
        pltpu.VMEM((2, 4, 2, UNIT, FF), BF),
        pltpu.VMEM((2, 4, 2, DOWN, D), BF),
        pltpu.VMEM((UNIT, FF), BF),
        pltpu.VMEM((DOWN, D), BF),
        pltpu.VMEM((UNIT, FF), BF),
        pltpu.VMEM((DOWN, D), BF),
        pltpu.VMEM((HALF, FF), BF),
        pltpu.VMEM((HALF, FF), BF),
        dma((N_E,)), dma((N_E,)), dma((N_E,)), dma((N_E,)), dma((N_E,)), dma((N_E,)),
        dma, dma,
        dma((2,)), dma((2,)),
        dma((2, 2, 4)), dma((2, 2, 4)),
        dma((2, N_Y)), dma((2, N_Y)),
        dma((2, N_Y)), dma((2, N_Y)),
        dma((2, 2, 4)), dma((2, 2, 4)),
        dma((2,)), dma((2,)),
        dma, dma,
    ]
    outs = pl.pallas_call(
        kernel,
        out_shape=(
            shape((TOK, D), BF), shape((TOK, 8), BF),
            shape((HALF, FF), BF), shape((HALF, FF), BF), shape((DOWN, D), BF),
        ),
        in_specs=[vmem] * 7,
        out_specs=(vmem,) * 5,
        scratch_shapes=scratch,
        compiler_params=pltpu.CompilerParams(
            collective_id=0, has_side_effects=True, vmem_limit_bytes=48 * 1024 * 1024
        ),
    )(tokens, out_grad, routes, gate_values, w_gate[0], w_up[0], w_down[0])
    token_grad, gate_grad, wg, wu, wd = outs
    return token_grad, gate_grad, wg[None], wu[None], wd[None]


def solution(mesh):
    rows = P(("dp", "expert"), None)
    weight = P("expert", "dp", None)
    return jax.shard_map(
        body,
        mesh=mesh,
        in_specs=(rows,) * 4 + (weight,) * 3,
        out_specs=(rows, rows, weight, weight, weight),
        check_vma=False,
    )
```

time: 534 us -> 89.9 us (0.17)
  waiting for transfers between devices: 454 us -> 0 us
  Pallas kernels: 0 us -> 81.3 us
  starting transfers between devices: 34.2 us -> 0 us
  matrix products: 19.2 us -> 0 us
  between operations: 14 us -> 0.67 us
    reduce_scatter x2 -> x0, waiting for transfers between devices: 205 us -> none  [the longest x1 127 us: body(): lax.psum_scatter(lax.dot_general(activation, scaled_grad, CONTRACT_ROWS,...]
    all_gather x3 -> x0, waiting for transfers between devices: 190 us -> none  [the longest x1 81.2 us: body(): lax.all_gather(w_up, 'dp', axis=1, tiled=True)]
    pallas_call x0 -> x1, Pallas kernels: none -> 81.3 us  [body(): pl.pallas_call(kernel, out_shape=(shape((TOK, D), BF), shape((TOK, 8), BF...]
    all_to_all x5 -> x0, waiting for transfers between devices: 57.2 us -> none  [the longest x1 17.3 us: body(): lax.all_to_all(input_grad.reshape(expert_count, capacity, features), 'exp...]
    all_to_all x5 -> x0, starting transfers between devices: 34 us -> none  [the longest x1 11.9 us: body(): lax.all_to_all(send_gates, 'expert', split_axis=0, concat_axis=0, tiled=T...]
    dot_general x13 -> x0, matrix products: 19.2 us -> none  [the longest x1 2.7 us: body(): lax.dot_general(activation, scaled_grad, CONTRACT_ROWS, preferred_element...]
    unnamed x12 -> x21, local copies, waits for them, and re-layouts: 0.81 us -> 7.52 us
  transfers between devices with their start and end apart: 10 -> 0, of which waited for: 10 -> 0; matrix products, arithmetic and copies ran while one was open for 4% -> 0% of each run, Pallas kernels for 0% -> 0%
where the time goes in v1:
time: 89.9 us; the launch traced here: 89.5 us
  Pallas kernels  81.3 us (90%)
  local copies, waits for them, and re-layouts  7.52 us (8%)
    pallas_call x1, Pallas kernels, body(): pl.pallas_call(kernel, out_shape=(shape((TOK, D), BF), shape((TOK, 8), BF...  81.3 us
    unnamed x21, local copies, waits for them, and re-layouts  7.52 us

profile of v1, /device:TPU:1, one launch (start us, length us, event | category | flops | bytes accessed | tf_op | source)
XLA Modules:
  0.0 89.5 jit_solution(9917472890586747919)
XLA Ops:
  0.6 0.0 copy-start.6
  0.6 0.0 copy-start.5
  0.7 0.7 copy-done.6
  1.3 0.0 copy-start.3
  1.3 0.1 copy.13.gates
  1.4 0.0 copy-done.5
  1.4 0.0 copy-start.2
  1.5 0.1 copy.12.routes
  1.6 0.5 copy-done.3
  2.1 0.1 copy-done.2
  2.2 0.0 copy-start
  2.2 1.0 %copy-done = bf16[128,1280]{1,0:T(8,128)(2,1)S(1)} copy-done((bf16[128,1280]{1,0:T(8,128)(2,1)S(1)}, bf16[128,1280]{1,0:T(8,128)(2,1)}, u32[]{:S(2)}) %copy-start) | copy-done | bytes 327704
  3.2 0.0 copy-start.1
  3.2 1.0 %copy-done.1 = bf16[128,1280]{1,0:T(8,128)(2,1)S(1)} copy-done((bf16[128,1280]{1,0:T(8,128)(2,1)S(1)}, bf16[128,1280]{1,0:T(8,128)(2,1)}, u32[]{:S(2)}) %copy-start.1) | copy-done | bytes 327704
  4.2 0.0 copy-start.4
  4.2 0.8 copy-done.4
  5.0 81.3 %shard_map.110 = (bf16[128,1280]{1,0:T(8,128)(2,1)S(1)}, bf16[128,8]{1,0:T(8,128)(2,1)S(1)}, bf16[40,512]{1,0:T(8,128)(2,1)S(1)}, bf16[40,512]{1,0:T(8,128)(2,1)S(1)}, bf16[16,1280]{1,0:T(8,128)(2,1)S(1)}) custom-call(bf16[128,1280]{1,0:T(8,128)(2,1)S(1)} %copy-done, bf16[128,1280]{1,0:T(8,128)(2,1)S(1)} %copy-done.1, s32[128,8]{1,0:T(8,128)S(1)} %copy.12.routes, ...), custom_call_target="tpu_custom_call" | custom-call | tf_op jit(solution)/shard_map/pallas_call | solution.py:384
  86.3 0.7 copy.14
  86.9 0.7 copy.19
  87.7 0.6 copy.20
  88.3 0.6 copy.21
  88.9 0.6 copy.22
Async XLA Ops:
  0.6 0.7 copy-start.6
  0.6 0.8 copy-start.5
  1.3 0.8 copy-start.3
  1.4 0.8 copy-start.2
  2.2 1.0 %copy-start = (bf16[128,1280]{1,0:T(8,128)(2,1)S(1)}, bf16[128,1280]{1,0:T(8,128)(2,1)}, u32[]{:S(2)}) copy-start(bf16[128,1280]{1,0:T(8,128)(2,1)} %tokens.1) | copy-start | bytes 983044
  3.2 1.0 %copy-start.1 = (bf16[128,1280]{1,0:T(8,128)(2,1)S(1)}, bf16[128,1280]{1,0:T(8,128)(2,1)}, u32[]{:S(2)}) copy-start(bf16[128,1280]{1,0:T(8,128)(2,1)} %grads.1) | copy-start | bytes 983044
  4.2 0.8 copy-start.4

commit v2 on v1

v2 whole, which is shorter than its diff:
```python
import jax
import jax.numpy as jnp
from jax import lax
from jax.experimental import pallas as pl
from jax.experimental.pallas import tpu as pltpu
from jax.sharding import PartitionSpec as P

EXP_DEV = 8
MESH = pl.DeviceIdType.MESH
BF = jnp.bfloat16
F32 = jnp.float32
ROWS = (((0,), (0,)), ((), ()))
LAST = (((1,), (1,)), ((), ()))

N_E = 16
N_Y = 8
TOK = 128
CAP = 16
SLOTS = N_E * CAP
D = 1280
FF = 512
WIDE = D + 128
UNIT = 40
DOWN = 16
STEPS = ((4, 3), (3, 4), (4, 3))


def kernel(
    tokens_hbm, grads_hbm, routes_hbm, gates_hbm, wg_hbm, wu_hbm, wd_hbm,
    tok_out, gate_out, wg_out, wu_out, wd_out,
    tokens, grads, routes, gates,
    place_ref, send_x, send_g, send_s, got_x, got_g, got_s, ret, back,
    w_all, wdn, w_mat,
    hu_ref, g_ref, a_ref, dhu_ref, e_ref,
    d2, dd, s2, sd, snd2, sndd, rec2, recd, xq_out, xq_in, xw_out, xw_in,
    loc, ss, rs, sx, rx, sg, rg, sr, rr, sxw, rxw, sxd, rxd, sag, rag, ssw, rsw,
    ssd, rsd, srs, rrs, sxq, rxq, sxr, rxr,
):
    dp = lax.axis_index("dp")
    ex = lax.axis_index("expert")
    core = lax.rem(dp, 2)
    xh = lax.rem(lax.div(dp, 2), 2)
    y = lax.div(dp, 4)
    other = 1 - core
    across = 1 - xh
    low = lax.rem(dp, 4)
    sibling = (dp + 1 - 2 * core, ex)
    partner = (dp + 2 - 4 * xh, ex)
    ups = (
        (lax.rem(y + 1, N_Y) * 4 + low, ex),
        (lax.rem(y + N_Y - 1, N_Y) * 4 + low, ex),
    )

    def wrap(offset):
        return lax.rem(y + (offset + 2 * N_Y), N_Y)

    def peer(k):
        return lax.rem(ex + (k + N_E), N_E)

    started = []

    def go(src, dst, send, recv, to):
        copy = pltpu.make_async_remote_copy(
            src_ref=src, dst_ref=dst, send_sem=send, recv_sem=recv,
            device_id=to, device_id_type=MESH,
        )
        copy.start()
        started.append(copy)
        return copy

    barrier = pltpu.get_barrier_semaphore()
    for to in (sibling, partner) + ups:
        pl.semaphore_signal(barrier, inc=1, device_id=to, device_id_type=MESH)
    for k in range(1, N_E):
        pl.semaphore_signal(barrier, inc=1, device_id=(dp, peer(k)), device_id_type=MESH)

    local = []
    for i, (src, dst) in enumerate((
        (routes_hbm, routes), (gates_hbm, gates), (tokens_hbm, tokens),
        (wg_hbm.at[0], w_all.at[y, xh, core, :, pl.ds(0, FF)]),
        (wu_hbm.at[0], w_all.at[y, xh, core, :, pl.ds(FF, FF)]),
        (wd_hbm.at[0], wdn.at[y, xh, core]), (grads_hbm, grads),
    )):
        local.append(pltpu.make_async_copy(src, dst, loc.at[i]))
        local[-1].start()

    line = lax.broadcasted_iota(jnp.int32, (SLOTS, TOK), 0)
    expert_id = lax.div(line, CAP) * EXP_DEV
    slot_id = lax.rem(line, CAP)
    before = (
        lax.broadcasted_iota(jnp.int32, (TOK, TOK), 0)
        < lax.broadcasted_iota(jnp.int32, (TOK, TOK), 1)
    )
    before = jnp.where(before, 1.0, 0.0).astype(BF)
    local[0].wait()
    local[1].wait()
    route = routes[...]
    gate_wide = gates[...].astype(F32)
    chosen = jnp.zeros((SLOTS, TOK), F32)
    gate_tok = jnp.zeros((SLOTS, TOK), F32)
    for k in range(8):
        match = route[k : k + 1] == expert_id
        chosen = jnp.where(match, 1.0, chosen)
        gate_tok = jnp.where(match, gate_wide[k : k + 1], gate_tok)
    rank = jnp.dot(chosen.astype(BF), before, preferred_element_type=F32)
    placing = jnp.where(rank == slot_id.astype(F32), chosen, 0.0)
    gate_column = jnp.sum(placing * gate_tok, axis=1, keepdims=True)
    placing = placing.astype(BF)
    place_ref[...] = placing
    local[2].wait()
    send_x[...] = (
        jnp.dot(placing, tokens[...], preferred_element_type=F32)
        .astype(BF).reshape(N_E, CAP, D)
    )
    gate_rows = jnp.broadcast_to(gate_column, (SLOTS, 128)).reshape(N_E, CAP, 128)
    diagonal = (
        lax.broadcasted_iota(jnp.int32, (CAP, 128), 0)
        == lax.broadcasted_iota(jnp.int32, (CAP, 128), 1)
    )
    send_s[...] = jnp.sum(jnp.where(diagonal[None], gate_rows, 0.0), axis=1, keepdims=True)
    for i in range(3, 6):
        local[i].wait()

    pl.semaphore_wait(barrier, 4 + N_E - 1)

    def block(piece, at):
        if piece < 2:
            return w_all.at[at, xh if piece == 0 else across, core]
        return wdn.at[at, xh if piece == 2 else across, core]

    def ring_send(piece, way, step):
        at = block(piece, wrap(-step if way == 0 else step))
        return go(at, at, sag.at[piece, way, step], rag.at[piece, way, step], ups[way])

    shared = []

    def to_sibling(piece, offset, index):
        at = block(piece, wrap(offset))
        shared.append(go(at, at, ssw.at[piece, index], rsw.at[piece, index], sibling))

    def to_partner(offset, index):
        at = block(2, wrap(offset))
        return go(at, at, sxd.at[index], rxd.at[index], partner)

    ring = {}
    crossed = {}
    for way in range(2):
        ring[0, way] = ring_send(0, way, 0)
    mine = block(0, y)
    part = go(mine, mine, sxw, rxw, partner)
    for way in range(2):
        ring[2, way] = ring_send(2, way, 0)
    row_x = [
        go(send_x.at[peer(k)], got_x.at[ex], sx.at[k], rx.at[k], (dp, peer(k)))
        for k in range(1, N_E)
    ]
    crossed[0] = to_partner(0, 0)
    to_sibling(0, 0, 0)
    to_sibling(2, 0, 0)
    got_x[ex] = send_x[ex]
    row_s = [
        go(send_s.at[peer(k)], got_s.at[ex], ss.at[k], rs.at[k], (dp, peer(k)))
        for k in range(1, N_E)
    ]
    got_s[ex] = send_s[ex]

    local[6].wait()
    send_g[...] = (
        jnp.dot(placing, grads[...], preferred_element_type=F32)
        .astype(BF).reshape(N_E, CAP, D)
    )
    got_g[ex] = send_g[ex]

    part.wait_recv()
    for way in range(2):
        ring[1, way] = ring_send(1, way, 0)
    row_g = [
        go(send_g.at[peer(k)], got_g.at[ex], sg.at[k], rg.at[k], (dp, peer(k)))
        for k in range(1, N_E)
    ]
    to_sibling(1, 0, 0)

    late = [(0, 0)]
    for step in range(4):
        fresh = []
        for piece in range(3):
            for way in range(2):
                if step < STEPS[piece][way]:
                    ring[piece, way].wait_recv()
                    if step + 1 < STEPS[piece][way]:
                        ring[piece, way] = ring_send(piece, way, step + 1)
                    offset = -1 - step if way == 0 else 1 + step
                    index = 1 + step if way == 0 else 1 + STEPS[piece][0] + step
                    if piece == 2:
                        crossed[index] = to_partner(offset, index)
                        fresh.append((offset, index))
                    to_sibling(piece, offset, index)
        for offset, index in late:
            crossed[index].wait_recv()
            to_sibling(3, offset, index)
        late = fresh
    for offset, index in late:
        crossed[index].wait_recv()
        to_sibling(3, offset, index)
    for copy in shared:
        copy.wait_recv()

    def flatten(i, carry):
        at = pl.ds(pl.multiple_of(i * 4 * UNIT, 4 * UNIT), 4 * UNIT)
        w_mat[at] = w_all[i].astype(F32).reshape(4 * UNIT, 2 * FF).astype(BF)
        return carry

    lax.fori_loop(0, N_Y, flatten, 0)
    for copy in row_x:
        copy.wait_recv()
    rows = got_x[...].reshape(SLOTS, D)
    hu_ref[...] = jnp.dot(rows, w_mat[...], preferred_element_type=F32)
    for copy in row_s:
        copy.wait_recv()
    for copy in row_g:
        copy.wait_recv()
    g_ref[...] = lax.dot_general(
        got_g[...].reshape(SLOTS, D), wdn[...].reshape(FF, D), LAST,
        preferred_element_type=F32,
    )

    def elementwise(i, carry):
        at = pl.ds(pl.multiple_of(i * CAP, CAP), CAP)
        h, u, g = hu_ref[at, :FF], hu_ref[at, FF:], g_ref[at]
        gate = jnp.sum(
            jnp.where(diagonal, jnp.broadcast_to(got_s[i], (CAP, 128)), 0.0),
            axis=1, keepdims=True,
        )
        s = jax.nn.sigmoid(h)
        a = (h * s * u).astype(BF)
        a_ref[at] = a
        term = jnp.sum(a.astype(F32) * g, axis=1, keepdims=True)
        ret[i, :, D:] = jnp.broadcast_to(term, (CAP, 128)).astype(BF)
        g = gate * g
        dhu_ref[at, :FF] = (g * u * s * (1.0 + h * (1.0 - s))).astype(BF)
        dhu_ref[at, FF:] = (g * h * s).astype(BF)
        e_ref[at] = (gate * got_g[i].astype(F32)).astype(BF)
        return carry

    lax.fori_loop(0, N_E, elementwise, 0)

    given = {}
    partial, paired = (d2, dd), (s2, sd)

    def give(kind, offset):
        at = wrap(offset)
        index = offset % N_Y
        given[kind, index] = go(
            partial[kind].at[at, :, other], paired[kind].at[at],
            ssd.at[kind, index], rsd.at[kind, index], sibling,
        )

    order = (4, -3, 3, 2, -2, 1, -1, 0)
    d2[...] = (
        lax.dot_general(rows, dhu_ref[...], ROWS, preferred_element_type=F32)
        .reshape(N_Y, 2, 2, UNIT, 2 * FF).astype(BF)
    )
    for offset in order:
        give(0, offset)
    dd[...] = (
        lax.dot_general(a_ref[...], e_ref[...], ROWS, preferred_element_type=F32)
        .astype(BF).reshape(N_Y, 2, 2, DOWN, D)
    )
    for offset in order:
        give(1, offset)

    arrived = set()

    def chip_sum(kind, offset, half):
        index = offset % N_Y
        if (kind, index) not in arrived:
            arrived.add((kind, index))
            given[kind, index].wait_recv()
        at = wrap(offset)
        return partial[kind][at, half, core].astype(F32) + paired[kind][at, half].astype(F32)

    def send_buf(piece, way, step):
        return snd2.at[piece, way, step] if piece < 2 else sndd.at[way, step]

    def recv_buf(piece, way, step):
        return rec2.at[piece, way, step] if piece < 2 else recd.at[way, step]

    going = {}
    swapped = {}

    def own_term(piece, offset):
        if piece == 0:
            return chip_sum(0, offset, across)
        if piece == 1:
            return chip_sum(0, offset, xh)
        swapped[offset % N_Y].wait_recv()
        return chip_sum(1, offset, xh) + xq_in[offset % N_Y].astype(F32)

    def reduce_step(piece, way, step):
        left = STEPS[piece][way] - step
        total = own_term(piece, left if way == 0 else -left)
        if step > 0:
            going[piece, way].wait_recv()
            total = total + recv_buf(piece, way, step - 1)[...].astype(F32)
        src = send_buf(piece, way, step)
        src[...] = total.astype(BF)
        going[piece, way] = go(
            src, recv_buf(piece, way, step),
            srs.at[piece, way, step], rrs.at[piece, way, step], ups[way],
        )

    for piece in range(2):
        for way in range(2):
            reduce_step(piece, way, 0)
    for offset in order:
        index = offset % N_Y
        xq_out[index] = chip_sum(1, offset, across).astype(BF)
        swapped[index] = go(
            xq_out.at[index], xq_in.at[index], sxq.at[index], rxq.at[index], partner
        )
    ret[:, :, :D] = (
        lax.dot_general(dhu_ref[...], w_mat[...], LAST, preferred_element_type=F32)
        .astype(BF).reshape(N_E, CAP, D)
    )
    back_rows = [
        go(ret.at[peer(k)], back.at[ex], sr.at[k], rr.at[k], (dp, peer(k)))
        for k in range(1, N_E)
    ]
    back[ex] = ret[ex]
    for step in range(1, 5):
        for piece in range(2):
            for way in range(2):
                if step < STEPS[piece][way]:
                    reduce_step(piece, way, step)
        for way in range(2):
            if step - 1 < STEPS[2][way]:
                reduce_step(2, way, step - 1)

    def ring_total(piece):
        total = own_term(piece, 0)
        for way in range(2):
            going[piece, way].wait_recv()
            total = total + recv_buf(piece, way, STEPS[piece][way] - 1)[...].astype(F32)
        return total

    xw_out[...] = ring_total(0).astype(BF)
    crossing = go(xw_out, xw_in, sxr, rxr, partner)
    kept = ring_total(1)
    wd_out[...] = ring_total(2).astype(BF)

    for copy in back_rows:
        copy.wait_recv()
    place = place_ref[...]
    tok_out[...] = lax.dot_general(
        place, back[:, :, :D].reshape(SLOTS, D), ROWS, preferred_element_type=F32
    ).astype(BF)
    terms = back[:, :, D:].reshape(SLOTS, 128)
    pick = lax.div(lax.broadcasted_iota(jnp.int32, (SLOTS, 128), 0), CAP)
    pick = pick == lax.broadcasted_iota(jnp.int32, (SLOTS, 128), 1)
    terms = jnp.where(pick, terms.astype(F32), 0.0).astype(BF)
    by_expert = lax.dot_general(terms, place, ROWS, preferred_element_type=F32)[:N_E]
    ids = lax.broadcasted_iota(jnp.int32, (N_E, TOK), 0) * EXP_DEV
    line = lax.broadcasted_iota(jnp.int32, (8, TOK), 0)
    result = jnp.zeros((8, TOK), F32)
    route = routes[...]
    for k in range(8):
        value = jnp.sum(
            jnp.where(route[k : k + 1] == ids, by_expert, 0.0), axis=0, keepdims=True
        )
        result = jnp.where(line == k, value, result)
    gate_out[...] = result.astype(BF)

    crossing.wait_recv()
    kept = (kept + xw_in[...].astype(F32)).astype(BF)
    wg_out[...] = kept[:, :FF]
    wu_out[...] = kept[:, FF:]
    for copy in started:
        copy.wait_send()


def body(tokens, out_grad, routes, gate_values, w_gate, w_up, w_down):
    anywhere = pl.BlockSpec(memory_space=pl.ANY)
    vmem = pl.BlockSpec(memory_space=pltpu.VMEM)
    dma = pltpu.SemaphoreType.DMA
    shape = jax.ShapeDtypeStruct
    scratch = [
        pltpu.VMEM((TOK, D), BF),
        pltpu.VMEM((TOK, D), BF),
        pltpu.VMEM((8, TOK), jnp.int32),
        pltpu.VMEM((8, TOK), BF),
        pltpu.VMEM((SLOTS, TOK), BF),
        pltpu.VMEM((N_E, CAP, D), BF),
        pltpu.VMEM((N_E, CAP, D), BF),
        pltpu.VMEM((N_E, 1, 128), F32),
        pltpu.VMEM((N_E, CAP, D), BF),
        pltpu.VMEM((N_E, CAP, D), BF),
        pltpu.VMEM((N_E, 1, 128), F32),
        pltpu.VMEM((N_E, CAP, WIDE), BF),
        pltpu.VMEM((N_E, CAP, WIDE), BF),
        pltpu.VMEM((N_Y, 2, 2, UNIT, 2 * FF), BF),
        pltpu.VMEM((N_Y, 2, 2, DOWN, D), BF),
        pltpu.VMEM((D, 2 * FF), BF),
        pltpu.VMEM((SLOTS, 2 * FF), F32),
        pltpu.VMEM((SLOTS, FF), F32),
        pltpu.VMEM((SLOTS, FF), BF),
        pltpu.VMEM((SLOTS, 2 * FF), BF),
        pltpu.VMEM((SLOTS, D), BF),
        pltpu.VMEM((N_Y, 2, 2, UNIT, 2 * FF), BF),
        pltpu.VMEM((N_Y, 2, 2, DOWN, D), BF),
        pltpu.VMEM((N_Y, 2, UNIT, 2 * FF), BF),
        pltpu.VMEM((N_Y, 2, DOWN, D), BF),
        pltpu.VMEM((2, 2, 4, UNIT, 2 * FF), BF),
        pltpu.VMEM((2, 4, DOWN, D), BF),
        pltpu.VMEM((2, 2, 4, UNIT, 2 * FF), BF),
        pltpu.VMEM((2, 4, DOWN, D), BF),
        pltpu.VMEM((N_Y, DOWN, D), BF),
        pltpu.VMEM((N_Y, DOWN, D), BF),
        pltpu.VMEM((UNIT, 2 * FF), BF),
        pltpu.VMEM((UNIT, 2 * FF), BF),
        dma((7,)),
        dma((N_E,)), dma((N_E,)), dma((N_E,)), dma((N_E,)),
        dma((N_E,)), dma((N_E,)), dma((N_E,)), dma((N_E,)),
        dma, dma,
        dma((N_Y,)), dma((N_Y,)),
        dma((3, 2, 4)), dma((3, 2, 4)),
        dma((4, N_Y)), dma((4, N_Y)),
        dma((2, N_Y)), dma((2, N_Y)),
        dma((3, 2, 4)), dma((3, 2, 4)),
        dma((N_Y,)), dma((N_Y,)),
        dma, dma,
    ]
    return pl.pallas_call(
        kernel,
        out_shape=(
            shape((TOK, D), BF), shape((8, TOK), BF),
            shape((UNIT, FF), BF), shape((UNIT, FF), BF), shape((DOWN, D), BF),
        ),
        in_specs=[anywhere] * 7,
        out_specs=(vmem,) * 5,
        scratch_shapes=scratch,
        compiler_params=pltpu.CompilerParams(
            collective_id=0, has_side_effects=True, vmem_limit_bytes=60 * 1024 * 1024
        ),
    )(tokens, out_grad, routes.T, gate_values.T, w_gate, w_up, w_down)


def solution(mesh):
    rows = P(("dp", "expert"), None)
    weight = P("expert", "dp", None)

    def whole(*args):
        token_grad, gate_grad, wg, wu, wd = body(*args)
        return token_grad, gate_grad.T, wg[None], wu[None], wd[None]

    return jax.shard_map(
        whole,
        mesh=mesh,
        in_specs=(rows,) * 4 + (weight,) * 3,
        out_specs=(rows, rows, weight, weight, weight),
        check_vma=False,
    )
```

time: 89.9 us -> 81 us (0.901)
  Pallas kernels: 81.3 us -> 75.5 us
  local copies, waits for them, and re-layouts: 7.52 us -> 4.52 us
    pallas_call x1, Pallas kernels: 81.3 us -> 75.5 us  [body(): pl.pallas_call(kernel, out_shape=(shape((TOK, D), BF), shape((8, TOK), BF...]
    unnamed x21 -> x13, local copies, waits for them, and re-layouts: 7.52 us -> 4.52 us
where the time goes in v2:
time: 81 us; the launch traced here: 80.7 us
  Pallas kernels  75.5 us (93%)
  local copies, waits for them, and re-layouts  4.52 us (6%)
    pallas_call x1, Pallas kernels, body(): pl.pallas_call(kernel, out_shape=(shape((TOK, D), BF), shape((8, TOK), BF...  75.5 us
    unnamed x13, local copies, waits for them, and re-layouts  4.52 us

profile of v2, /device:TPU:1, one launch (start us, length us, event | category | flops | bytes accessed | tf_op | source)
XLA Modules:
  0.0 80.7 jit_solution(3656372387694679740)
XLA Ops:
  0.6 75.5 %shard_map.110 = (bf16[128,1280]{1,0:T(8,128)(2,1)}, bf16[8,128]{1,0:T(8,128)(2,1)}, bf16[40,512]{1,0:T(8,128)(2,1)}, bf16[40,512]{1,0:T(8,128)(2,1)}, bf16[16,1280]{1,0:T(8,128)(2,1)}) custom-call(bf16[128,1280]{1,0:T(8,128)(2,1)} %tokens_hbm.1, bf16[128,1280]{1,0:T(8,128)(2,1)} %grads_hbm.1, s32[8,128]{1,0:T(8,128)} %bitcast.9, bf16[8,128]{1,0:T(8,128)(2,1)} %bitcast.10, ...), custom_call_target="tpu_custom_call" | custom-call | tf_op jit(solution)/shard_map/pallas_call | solution.py:432
  76.1 0.0 copy-start.3
  76.1 0.0 copy-start.2
  76.2 1.7 %copy.17 = bf16[128,1280]{1,0:T(8,128)(2,1)} copy(bf16[128,1280]{1,0:T(8,128)(2,1)} %get-tuple-element.20) | data formatting | bytes 655360
  77.9 0.0 copy-done.3
  77.9 0.6 copy.18
  78.5 0.0 copy-done.2
  78.5 0.0 copy-start.1
  78.5 0.6 copy.19
  79.1 0.2 copy-done.1
  79.3 0.0 copy-start
  79.3 0.6 copy.20
  79.9 0.2 copy-done
  80.1 0.6 copy.21
Async XLA Ops:
  76.1 1.7 %copy-start.3 = (bf16[8,128]{1,0:T(8,128)(2,1)S(1)}, bf16[8,128]{1,0:T(8,128)(2,1)}, u32[]{:S(2)}) copy-start(bf16[8,128]{1,0:T(8,128)(2,1)} %get-tuple-element.11) | copy-start | bytes 6148
  76.1 2.3 %copy-start.2 = (bf16[40,512]{1,0:T(8,128)(2,1)S(1)}, bf16[40,512]{1,0:T(8,128)(2,1)}, u32[]{:S(2)}) copy-start(bf16[40,512]{1,0:T(8,128)(2,1)} %get-tuple-element.12) | copy-start | bytes 122884
  78.5 0.8 copy-start.1
  79.3 0.8 copy-start

commit v3 on v2

--- a/solution.py
+++ b/solution.py
@@ -22,15 +22,19 @@
 WIDE = D + 128
 UNIT = 40
 DOWN = 16
+PEERS = (8, 7, 9, 6, 10, 5, 11, 4, 12, 3, 13, 2, 14, 1, 15)
 STEPS = ((4, 3), (3, 4), (4, 3))
+PARTS = ((4, 3), (4, 3), (3, 4), (3, 4), (3, 4))
+LAST_IN = 3
 
 
 def kernel(
     tokens_hbm, grads_hbm, routes_hbm, gates_hbm, wg_hbm, wu_hbm, wd_hbm,
+    tok_hbm, gate_hbm, wg_out_hbm, wu_out_hbm, wd_out_hbm,
     tok_out, gate_out, wg_out, wu_out, wd_out,
     tokens, grads, routes, gates,
     place_ref, send_x, send_g, send_s, got_x, got_g, got_s, ret, back,
-    w_all, wdn, w_mat,
+    w_all, wdn, w_mat, xt_ref, wdt_ref,
     hu_ref, g_ref, a_ref, dhu_ref, e_ref,
     d2, dd, s2, sd, snd2, sndd, rec2, recd, xq_out, xq_in, xw_out, xw_in,
     loc, ss, rs, sx, rx, sg, rg, sr, rr, sxw, rxw, sxd, rxd, sag, rag, ssw, rsw,
@@ -68,6 +72,12 @@
         started.append(copy)
         return copy
 
+    leaving = []
+
+    def leave(i, src, dst):
+        leaving.append(pltpu.make_async_copy(src, dst, loc.at[7 + i]))
+        leaving[-1].start()
+
     barrier = pltpu.get_barrier_semaphore()
     for to in (sibling, partner) + ups:
         pl.semaphore_signal(barrier, inc=1, device_id=to, device_id_type=MESH)
@@ -93,35 +103,28 @@
     )
     before = jnp.where(before, 1.0, 0.0).astype(BF)
     local[0].wait()
-    local[1].wait()
     route = routes[...]
-    gate_wide = gates[...].astype(F32)
     chosen = jnp.zeros((SLOTS, TOK), F32)
-    gate_tok = jnp.zeros((SLOTS, TOK), F32)
     for k in range(8):
         match = route[k : k + 1] == expert_id
         chosen = jnp.where(match, 1.0, chosen)
-        gate_tok = jnp.where(match, gate_wide[k : k + 1], gate_tok)
     rank = jnp.dot(chosen.astype(BF), before, preferred_element_type=F32)
     placing = jnp.where(rank == slot_id.astype(F32), chosen, 0.0)
-    gate_column = jnp.sum(placing * gate_tok, axis=1, keepdims=True)
     placing = placing.astype(BF)
-    place_ref[...] = placing
     local[2].wait()
     send_x[...] = (
         jnp.dot(placing, tokens[...], preferred_element_type=F32)
         .astype(BF).reshape(N_E, CAP, D)
     )
-    gate_rows = jnp.broadcast_to(gate_column, (SLOTS, 128)).reshape(N_E, CAP, 128)
-    diagonal = (
-        lax.broadcasted_iota(jnp.int32, (CAP, 128), 0)
-        == lax.broadcasted_iota(jnp.int32, (CAP, 128), 1)
-    )
-    send_s[...] = jnp.sum(jnp.where(diagonal[None], gate_rows, 0.0), axis=1, keepdims=True)
+
+    pl.semaphore_wait(barrier, 4 + N_E - 1)
+
+    row_x = [
+        go(send_x.at[peer(k)], got_x.at[ex], sx.at[k], rx.at[k], (dp, peer(k)))
+        for k in PEERS
+    ]
     for i in range(3, 6):
         local[i].wait()
-
-    pl.semaphore_wait(barrier, 4 + N_E - 1)
 
     def block(piece, at):
         if piece < 2:
@@ -150,17 +153,26 @@
     part = go(mine, mine, sxw, rxw, partner)
     for way in range(2):
         ring[2, way] = ring_send(2, way, 0)
-    row_x = [
-        go(send_x.at[peer(k)], got_x.at[ex], sx.at[k], rx.at[k], (dp, peer(k)))
-        for k in range(1, N_E)
-    ]
     crossed[0] = to_partner(0, 0)
     to_sibling(0, 0, 0)
     to_sibling(2, 0, 0)
     got_x[ex] = send_x[ex]
+    place_ref[...] = placing
+    local[1].wait()
+    gate_wide = gates[...].astype(F32)
+    gate_tok = jnp.zeros((SLOTS, TOK), F32)
+    for k in range(8):
+        gate_tok = jnp.where(route[k : k + 1] == expert_id, gate_wide[k : k + 1], gate_tok)
+    gate_column = jnp.sum(placing.astype(F32) * gate_tok, axis=1, keepdims=True)
+    gate_rows = jnp.broadcast_to(gate_column, (SLOTS, 128)).reshape(N_E, CAP, 128)
+    diagonal = (
+        lax.broadcasted_iota(jnp.int32, (CAP, 128), 0)
+        == lax.broadcasted_iota(jnp.int32, (CAP, 128), 1)
+    )
+    send_s[...] = jnp.sum(jnp.where(diagonal[None], gate_rows, 0.0), axis=1, keepdims=True)
     row_s = [
         go(send_s.at[peer(k)], got_s.at[ex], ss.at[k], rs.at[k], (dp, peer(k)))
-        for k in range(1, N_E)
+        for k in PEERS
     ]
     got_s[ex] = send_s[ex]
 
@@ -176,7 +188,7 @@
         ring[1, way] = ring_send(1, way, 0)
     row_g = [
         go(send_g.at[peer(k)], got_g.at[ex], sg.at[k], rg.at[k], (dp, peer(k)))
-        for k in range(1, N_E)
+        for k in PEERS
     ]
     to_sibling(1, 0, 0)
 
@@ -215,16 +227,18 @@
         copy.wait_recv()
     rows = got_x[...].reshape(SLOTS, D)
     hu_ref[...] = jnp.dot(rows, w_mat[...], preferred_element_type=F32)
+    xt_ref[...] = rows.T
+    wdt_ref[...] = wdn[...].reshape(FF, D).T
     for copy in row_s:
         copy.wait_recv()
-    for copy in row_g:
-        copy.wait_recv()
-    g_ref[...] = lax.dot_general(
-        got_g[...].reshape(SLOTS, D), wdn[...].reshape(FF, D), LAST,
-        preferred_element_type=F32,
-    )
-
-    def elementwise(i, carry):
+
+    def act_grad(sources):
+        got = jnp.concatenate([got_g[i] for i in sources], axis=0)
+        g = jnp.dot(got, wdt_ref[...], preferred_element_type=F32)
+        for n, i in enumerate(sources):
+            g_ref[pl.ds(pl.multiple_of(i * CAP, CAP), CAP)] = g[n * CAP : (n + 1) * CAP]
+
+    def elementwise(i):
         at = pl.ds(pl.multiple_of(i * CAP, CAP), CAP)
         h, u, g = hu_ref[at, :FF], hu_ref[at, FF:], g_ref[at]
         gate = jnp.sum(
@@ -240,9 +254,22 @@
         dhu_ref[at, :FF] = (g * u * s * (1.0 + h * (1.0 - s))).astype(BF)
         dhu_ref[at, FF:] = (g * h * s).astype(BF)
         e_ref[at] = (gate * got_g[i].astype(F32)).astype(BF)
+
+    def turn(n, carry):
+        k = 8 + lax.div(n + 1, 2) * (1 - 2 * lax.rem(n, 2))
+        elementwise(lax.rem(ex + N_E - k, N_E))
         return carry
 
-    lax.fori_loop(0, N_E, elementwise, 0)
+    early = N_E - 1 - LAST_IN
+    for copy in row_g[:early]:
+        copy.wait_recv()
+    act_grad([ex] + [peer(-k) for k in PEERS[:early]])
+    elementwise(ex)
+    lax.fori_loop(0, early, turn, 0)
+    for copy in row_g[early:]:
+        copy.wait_recv()
+    act_grad([peer(-k) for k in PEERS[early:]])
+    lax.fori_loop(early, N_E - 1, turn, 0)
 
     given = {}
     partial, paired = (d2, dd), (s2, sd)
@@ -256,48 +283,51 @@
         )
 
     order = (4, -3, 3, 2, -2, 1, -1, 0)
-    d2[...] = (
-        lax.dot_general(rows, dhu_ref[...], ROWS, preferred_element_type=F32)
-        .reshape(N_Y, 2, 2, UNIT, 2 * FF).astype(BF)
-    )
-    for offset in order:
-        give(0, offset)
     dd[...] = (
         lax.dot_general(a_ref[...], e_ref[...], ROWS, preferred_element_type=F32)
         .astype(BF).reshape(N_Y, 2, 2, DOWN, D)
     )
     for offset in order:
         give(1, offset)
+    for offset in order:
+        at = wrap(offset)
+        d2[at] = (
+            jnp.dot(
+                xt_ref[pl.ds(pl.multiple_of(at * 4 * UNIT, 4 * UNIT), 4 * UNIT)], dhu_ref[...],
+                preferred_element_type=F32,
+            ).reshape(2, 2, UNIT, 2 * FF).astype(BF)
+        )
+        give(0, offset)
 
     arrived = set()
 
-    def chip_sum(kind, offset, half):
+    def chip_sum(kind, offset, half, lanes=slice(None)):
         index = offset % N_Y
         if (kind, index) not in arrived:
             arrived.add((kind, index))
             given[kind, index].wait_recv()
         at = wrap(offset)
-        return partial[kind][at, half, core].astype(F32) + paired[kind][at, half].astype(F32)
+        own, came = partial[kind], paired[kind]
+        return own[at, half, core, :, lanes].astype(F32) + came[at, half, :, lanes].astype(F32)
 
     def send_buf(piece, way, step):
-        return snd2.at[piece, way, step] if piece < 2 else sndd.at[way, step]
+        return snd2.at[piece, way, step] if piece < 4 else sndd.at[way, step]
 
     def recv_buf(piece, way, step):
-        return rec2.at[piece, way, step] if piece < 2 else recd.at[way, step]
+        return rec2.at[piece, way, step] if piece < 4 else recd.at[way, step]
 
     going = {}
     swapped = {}
 
     def own_term(piece, offset):
-        if piece == 0:
-            return chip_sum(0, offset, across)
-        if piece == 1:
-            return chip_sum(0, offset, xh)
+        if piece < 4:
+            lanes = slice(0, FF) if piece % 2 == 0 else slice(FF, 2 * FF)
+            return chip_sum(0, offset, across if piece < 2 else xh, lanes)
         swapped[offset % N_Y].wait_recv()
         return chip_sum(1, offset, xh) + xq_in[offset % N_Y].astype(F32)
 
     def reduce_step(piece, way, step):
-        left = STEPS[piece][way] - step
+        left = PARTS[piece][way] - step
         total = own_term(piece, left if way == 0 else -left)
         if step > 0:
             going[piece, way].wait_recv()
@@ -312,41 +342,49 @@
     for piece in range(2):
         for way in range(2):
             reduce_step(piece, way, 0)
-    for offset in order:
+    for offset in (3, -4, 2, -3, 1, -2, -1, 0):
         index = offset % N_Y
         xq_out[index] = chip_sum(1, offset, across).astype(BF)
         swapped[index] = go(
             xq_out.at[index], xq_in.at[index], sxq.at[index], rxq.at[index], partner
         )
+    for piece in range(2, 4):
+        for way in range(2):
+            reduce_step(piece, way, 0)
     ret[:, :, :D] = (
         lax.dot_general(dhu_ref[...], w_mat[...], LAST, preferred_element_type=F32)
         .astype(BF).reshape(N_E, CAP, D)
     )
     back_rows = [
         go(ret.at[peer(k)], back.at[ex], sr.at[k], rr.at[k], (dp, peer(k)))
-        for k in range(1, N_E)
+        for k in PEERS
     ]
     back[ex] = ret[ex]
-    for step in range(1, 5):
-        for piece in range(2):
+    for step in range(4):
+        for piece in range(4):
             for way in range(2):
-                if step < STEPS[piece][way]:
+                if 0 < step < PARTS[piece][way]:
                     reduce_step(piece, way, step)
         for way in range(2):
-            if step - 1 < STEPS[2][way]:
-                reduce_step(2, way, step - 1)
+            if step < PARTS[4][way]:
+                reduce_step(4, way, step)
 
     def ring_total(piece):
         total = own_term(piece, 0)
         for way in range(2):
             going[piece, way].wait_recv()
-            total = total + recv_buf(piece, way, STEPS[piece][way] - 1)[...].astype(F32)
+            total = total + recv_buf(piece, way, PARTS[piece][way] - 1)[...].astype(F32)
         return total
 
-    xw_out[...] = ring_total(0).astype(BF)
-    crossing = go(xw_out, xw_in, sxr, rxr, partner)
-    kept = ring_total(1)
-    wd_out[...] = ring_total(2).astype(BF)
+    crossing = []
+    for piece in range(2):
+        xw_out[piece] = ring_total(piece).astype(BF)
+        crossing.append(
+            go(xw_out.at[piece], xw_in.at[piece], sxr.at[piece], rxr.at[piece], partner)
+        )
+    kept = [ring_total(2), ring_total(3)]
+    wd_out[...] = ring_total(4).astype(BF)
+    leave(4, wd_out, wd_out_hbm)
 
     for copy in back_rows:
         copy.wait_recv()
@@ -354,6 +392,7 @@
     tok_out[...] = lax.dot_general(
         place, back[:, :, :D].reshape(SLOTS, D), ROWS, preferred_element_type=F32
     ).astype(BF)
+    leave(0, tok_out, tok_hbm)
     terms = back[:, :, D:].reshape(SLOTS, 128)
     pick = lax.div(lax.broadcasted_iota(jnp.int32, (SLOTS, 128), 0), CAP)
     pick = pick == lax.broadcasted_iota(jnp.int32, (SLOTS, 128), 1)
@@ -369,13 +408,22 @@
         )
         result = jnp.where(line == k, value, result)
     gate_out[...] = result.astype(BF)
-
-    crossing.wait_recv()
-    kept = (kept + xw_in[...].astype(F32)).astype(BF)
-    wg_out[...] = kept[:, :FF]
-    wu_out[...] = kept[:, FF:]
+    leave(1, gate_out, gate_hbm)
+
+    for piece, out in enumerate((wg_out, wu_out)):
+        crossing[piece].wait_recv()
+        out[...] = (kept[piece] + xw_in[piece].astype(F32)).astype(BF)
+    leave(2, wg_out, wg_out_hbm)
+    leave(3, wu_out, wu_out_hbm)
+    for copy in leaving:
+        copy.wait()
     for copy in started:
         copy.wait_send()
+
+
+def hand_over(*refs):
+    for i in range(5):
+        refs[5 + i][...] = refs[i][...].reshape(refs[5 + i].shape)
 
 
 def body(tokens, out_grad, routes, gate_values, w_gate, w_up, w_down):
@@ -384,6 +432,11 @@
     dma = pltpu.SemaphoreType.DMA
     shape = jax.ShapeDtypeStruct
     scratch = [
+        pltpu.VMEM((TOK, D), BF),
+        pltpu.VMEM((8, TOK), BF),
+        pltpu.VMEM((UNIT, FF), BF),
+        pltpu.VMEM((UNIT, FF), BF),
+        pltpu.VMEM((DOWN, D), BF),
         pltpu.VMEM((TOK, D), BF),
         pltpu.VMEM((TOK, D), BF),
         pltpu.VMEM((8, TOK), jnp.int32),
@@ -400,6 +453,8 @@
         pltpu.VMEM((N_Y, 2, 2, UNIT, 2 * FF), BF),
         pltpu.VMEM((N_Y, 2, 2, DOWN, D), BF),
         pltpu.VMEM((D, 2 * FF), BF),
+        pltpu.VMEM((D, SLOTS), BF),
+        pltpu.VMEM((D, FF), BF),
         pltpu.VMEM((SLOTS, 2 * FF), F32),
         pltpu.VMEM((SLOTS, FF), F32),
         pltpu.VMEM((SLOTS, FF), BF),
@@ -409,15 +464,15 @@
         pltpu.VMEM((N_Y, 2, 2, DOWN, D), BF),
         pltpu.VMEM((N_Y, 2, UNIT, 2 * FF), BF),
         pltpu.VMEM((N_Y, 2, DOWN, D), BF),
-        pltpu.VMEM((2, 2, 4, UNIT, 2 * FF), BF),
+        pltpu.VMEM((4, 2, 4, UNIT, FF), BF),
         pltpu.VMEM((2, 4, DOWN, D), BF),
-        pltpu.VMEM((2, 2, 4, UNIT, 2 * FF), BF),
+        pltpu.VMEM((4, 2, 4, UNIT, FF), BF),
         pltpu.VMEM((2, 4, DOWN, D), BF),
         pltpu.VMEM((N_Y, DOWN, D), BF),
         pltpu.VMEM((N_Y, DOWN, D), BF),
-        pltpu.VMEM((UNIT, 2 * FF), BF),
-        pltpu.VMEM((UNIT, 2 * FF), BF),
-        dma((7,)),
+        pltpu.VMEM((2, UNIT, FF), BF),
+        pltpu.VMEM((2, UNIT, FF), BF),
+        dma((12,)),
         dma((N_E,)), dma((N_E,)), dma((N_E,)), dma((N_E,)),
         dma((N_E,)), dma((N_E,)), dma((N_E,)), dma((N_E,)),
         dma, dma,
@@ -425,23 +480,32 @@
         dma((3, 2, 4)), dma((3, 2, 4)),
         dma((4, N_Y)), dma((4, N_Y)),
         dma((2, N_Y)), dma((2, N_Y)),
-        dma((3, 2, 4)), dma((3, 2, 4)),
+        dma((5, 2, 4)), dma((5, 2, 4)),
         dma((N_Y,)), dma((N_Y,)),
-        dma, dma,
+        dma((2,)), dma((2,)),
     ]
-    return pl.pallas_call(
+    outs = pl.pallas_call(
         kernel,
         out_shape=(
             shape((TOK, D), BF), shape((8, TOK), BF),
             shape((UNIT, FF), BF), shape((UNIT, FF), BF), shape((DOWN, D), BF),
         ),
         in_specs=[anywhere] * 7,
-        out_specs=(vmem,) * 5,
+        out_specs=(anywhere,) * 5,
         scratch_shapes=scratch,
         compiler_params=pltpu.CompilerParams(
             collective_id=0, has_side_effects=True, vmem_limit_bytes=60 * 1024 * 1024
         ),
     )(tokens, out_grad, routes.T, gate_values.T, w_gate, w_up, w_down)
+    return pl.pallas_call(
+        hand_over,
+        out_shape=(
+            shape((TOK, D), BF), shape((8, TOK), BF),
+            shape((1, UNIT, FF), BF), shape((1, UNIT, FF), BF), shape((1, DOWN, D), BF),
+        ),
+        in_specs=[vmem] * 5,
+        out_specs=(vmem,) * 5,
+    )(*outs)
 
 
 def solution(mesh):
@@ -450,7 +514,7 @@
 
     def whole(*args):
         token_grad, gate_grad, wg, wu, wd = body(*args)
-        return token_grad, gate_grad.T, wg[None], wu[None], wd[None]
+        return token_grad, gate_grad.T, wg, wu, wd
 
     return jax.shard_map(
         whole,

time: 81 us -> 78.6 us (0.970)
  local copies, waits for them, and re-layouts: 4.52 us -> 0 us
  Pallas kernels: 75.5 us -> 77.8 us
    unnamed x13 -> x0, local copies, waits for them, and re-layouts: 4.52 us -> none
    pallas_call x0 -> x1, Pallas kernels: none -> 1.77 us  [body(): pl.pallas_call(hand_over, out_shape=(shape((TOK, D), BF), shape((8, TOK),...]
where the time goes in v3:
time: 78.6 us; the launch traced here: 78.4 us
  Pallas kernels  77.8 us (99%)
    pallas_call x1, Pallas kernels, body(): pl.pallas_call(kernel, out_shape=(shape((TOK, D), BF), shape((8, TOK), BF...  76 us
    pallas_call x1, Pallas kernels, body(): pl.pallas_call(hand_over, out_shape=(shape((TOK, D), BF), shape((8, TOK),...  1.77 us

profile of v3, /device:TPU:1, one launch (start us, length us, event | category | flops | bytes accessed | tf_op | source)
XLA Modules:
  0.0 78.4 jit_solution(9794859208235724878)
XLA Ops:
  0.6 76.0 %shard_map.110 = (bf16[128,1280]{1,0:T(8,128)(2,1)}, bf16[8,128]{1,0:T(8,128)(2,1)}, bf16[40,512]{1,0:T(8,128)(2,1)}, bf16[40,512]{1,0:T(8,128)(2,1)}, bf16[16,1280]{1,0:T(8,128)(2,1)}) custom-call(bf16[128,1280]{1,0:T(8,128)(2,1)} %tokens_hbm.1, bf16[128,1280]{1,0:T(8,128)(2,1)} %grads_hbm.1, s32[8,128]{1,0:T(8,128)} %bitcast.3, bf16[8,128]{1,0:T(8,128)(2,1)} %bitcast.4, ...), custom_call_target="tpu_custom_call" | custom-call | tf_op jit(solution)/shard_map/pallas_call | solution.py:487
  76.6 1.8 %shard_map.111 = (bf16[128,1280]{1,0:T(8,128)(2,1)}, bf16[8,128]{1,0:T(8,128)(2,1)}, bf16[1,40,512]{2,1,0:T(8,128)(2,1)}, bf16[1,40,512]{2,1,0:T(8,128)(2,1)}, bf16[1,16,1280]{2,1,0:T(8,128)(2,1)}) custom-call(bf16[128,1280]{1,0:T(8,128)(2,1)} %get-tuple-element.15.refs_0_, bf16[8,128]{1,0:T(8,128)(2,1)} %get-tuple-element.16.refs_1_, ...), custom_call_target="tpu_custom_call" | custom-call | tf_op jit(solution)/shard_map/pallas_call | solution.py:500

commit v4 on v3

--- a/solution.py
+++ b/solution.py
@@ -19,12 +19,11 @@
 SLOTS = N_E * CAP
 D = 1280
 FF = 512
-WIDE = D + 128
 UNIT = 40
 DOWN = 16
 PEERS = (8, 7, 9, 6, 10, 5, 11, 4, 12, 3, 13, 2, 14, 1, 15)
 STEPS = ((4, 3), (3, 4), (4, 3))
-PARTS = ((4, 3), (4, 3), (3, 4), (3, 4), (3, 4))
+PARTS = ((3, 3), (3, 3), (3, 4), (3, 4), (3, 4))
 LAST_IN = 3
 
 
@@ -33,12 +32,12 @@
     tok_hbm, gate_hbm, wg_out_hbm, wu_out_hbm, wd_out_hbm,
     tok_out, gate_out, wg_out, wu_out, wd_out,
     tokens, grads, routes, gates,
-    place_ref, send_x, send_g, send_s, got_x, got_g, got_s, ret, back,
+    place_ref, send_x, send_g, send_s, got_x, got_g, got_s, ret, back, ret_s, back_s,
     w_all, wdn, w_mat, xt_ref, wdt_ref,
     hu_ref, g_ref, a_ref, dhu_ref, e_ref,
-    d2, dd, s2, sd, snd2, sndd, rec2, recd, xq_out, xq_in, xw_out, xw_in,
+    d2, dd, s2, sd, snd2, sndd, rec2, recd, xq_out, xq_in, xw_out, xw_in, far_out, far_in,
     loc, ss, rs, sx, rx, sg, rg, sr, rr, sxw, rxw, sxd, rxd, sag, rag, ssw, rsw,
-    ssd, rsd, srs, rrs, sxq, rxq, sxr, rxr,
+    ssd, rsd, srs, rrs, sxq, rxq, sxr, rxr, sfr, rfr, st, rt,
 ):
     dp = lax.axis_index("dp")
     ex = lax.axis_index("expert")
@@ -55,6 +54,9 @@
         (lax.rem(y + N_Y - 1, N_Y) * 4 + low, ex),
     )
 
+    up_two = (lax.rem(y + 2, N_Y) * 4 + low, ex)
+    down_two = (lax.rem(y + N_Y - 2, N_Y) * 4 + low, ex)
+
     def wrap(offset):
         return lax.rem(y + (offset + 2 * N_Y), N_Y)
 
@@ -79,7 +81,7 @@
         leaving[-1].start()
 
     barrier = pltpu.get_barrier_semaphore()
-    for to in (sibling, partner) + ups:
+    for to in (sibling, partner, down_two) + ups:
         pl.semaphore_signal(barrier, inc=1, device_id=to, device_id_type=MESH)
     for k in range(1, N_E):
         pl.semaphore_signal(barrier, inc=1, device_id=(dp, peer(k)), device_id_type=MESH)
@@ -94,9 +96,8 @@
         local.append(pltpu.make_async_copy(src, dst, loc.at[i]))
         local[-1].start()
 
-    line = lax.broadcasted_iota(jnp.int32, (SLOTS, TOK), 0)
-    expert_id = lax.div(line, CAP) * EXP_DEV
-    slot_id = lax.rem(line, CAP)
+    expert_id = EXP_DEV * lax.broadcasted_iota(jnp.int32, (N_E, CAP, TOK), 0).reshape(SLOTS, TOK)
+    slot_id = lax.broadcasted_iota(jnp.int32, (N_E, CAP, TOK), 1).reshape(SLOTS, TOK)
     before = (
         lax.broadcasted_iota(jnp.int32, (TOK, TOK), 0)
         < lax.broadcasted_iota(jnp.int32, (TOK, TOK), 1)
@@ -117,7 +118,7 @@
         .astype(BF).reshape(N_E, CAP, D)
     )
 
-    pl.semaphore_wait(barrier, 4 + N_E - 1)
+    pl.semaphore_wait(barrier, 5 + N_E - 1)
 
     row_x = [
         go(send_x.at[peer(k)], got_x.at[ex], sx.at[k], rx.at[k], (dp, peer(k)))
@@ -193,11 +194,12 @@
     to_sibling(1, 0, 0)
 
     late = [(0, 0)]
-    for step in range(4):
+    for turn_at in range(5):
         fresh = []
-        for piece in range(3):
+        for piece in (0, 2, 1):
+            step = turn_at - 1 if piece == 1 else turn_at
             for way in range(2):
-                if step < STEPS[piece][way]:
+                if 0 <= step < STEPS[piece][way]:
                     ring[piece, way].wait_recv()
                     if step + 1 < STEPS[piece][way]:
                         ring[piece, way] = ring_send(piece, way, step + 1)
@@ -249,7 +251,9 @@
         a = (h * s * u).astype(BF)
         a_ref[at] = a
         term = jnp.sum(a.astype(F32) * g, axis=1, keepdims=True)
-        ret[i, :, D:] = jnp.broadcast_to(term, (CAP, 128)).astype(BF)
+        ret_s[i] = jnp.sum(
+            jnp.where(diagonal, jnp.broadcast_to(term, (CAP, 128)), 0.0), axis=0, keepdims=True
+        )
         g = gate * g
         dhu_ref[at, :FF] = (g * u * s * (1.0 + h * (1.0 - s))).astype(BF)
         dhu_ref[at, FF:] = (g * h * s).astype(BF)
@@ -282,7 +286,7 @@
             ssd.at[kind, index], rsd.at[kind, index], sibling,
         )
 
-    order = (4, -3, 3, 2, -2, 1, -1, 0)
+    order = (4, 3, -3, 2, -2, 1, -1, 0)
     dd[...] = (
         lax.dot_general(a_ref[...], e_ref[...], ROWS, preferred_element_type=F32)
         .astype(BF).reshape(N_Y, 2, 2, DOWN, D)
@@ -332,6 +336,9 @@
         if step > 0:
             going[piece, way].wait_recv()
             total = total + recv_buf(piece, way, step - 1)[...].astype(F32)
+        if piece < 2 and way == 0 and step == 1:
+            far[piece].wait_recv()
+            total = total + far_in[piece].astype(F32)
         src = send_buf(piece, way, step)
         src[...] = total.astype(BF)
         going[piece, way] = go(
@@ -339,7 +346,11 @@
             srs.at[piece, way, step], rrs.at[piece, way, step], ups[way],
         )
 
+    far = []
     for piece in range(2):
+        lanes = slice(piece * FF, piece * FF + FF)
+        far_out[piece] = chip_sum(0, 4, across, lanes).astype(BF)
+        far.append(go(far_out.at[piece], far_in.at[piece], sfr.at[piece], rfr.at[piece], up_two))
         for way in range(2):
             reduce_step(piece, way, 0)
     for offset in (3, -4, 2, -3, 1, -2, -1, 0):
@@ -351,7 +362,7 @@
     for piece in range(2, 4):
         for way in range(2):
             reduce_step(piece, way, 0)
-    ret[:, :, :D] = (
+    ret[...] = (
         lax.dot_general(dhu_ref[...], w_mat[...], LAST, preferred_element_type=F32)
         .astype(BF).reshape(N_E, CAP, D)
     )
@@ -359,8 +370,27 @@
         go(ret.at[peer(k)], back.at[ex], sr.at[k], rr.at[k], (dp, peer(k)))
         for k in PEERS
     ]
+    back_terms = [
+        go(ret_s.at[peer(k)], back_s.at[ex], st.at[k], rt.at[k], (dp, peer(k)))
+        for k in PEERS
+    ]
     back[ex] = ret[ex]
+    back_s[ex] = ret_s[ex]
+    def ring_total(piece):
+        total = own_term(piece, 0)
+        for way in range(2):
+            going[piece, way].wait_recv()
+            total = total + recv_buf(piece, way, PARTS[piece][way] - 1)[...].astype(F32)
+        return total
+
+    crossing = []
     for step in range(4):
+        if step == 3:
+            for piece in range(2):
+                xw_out[piece] = ring_total(piece).astype(BF)
+                crossing.append(
+                    go(xw_out.at[piece], xw_in.at[piece], sxr.at[piece], rxr.at[piece], partner)
+                )
         for piece in range(4):
             for way in range(2):
                 if 0 < step < PARTS[piece][way]:
@@ -369,34 +399,27 @@
             if step < PARTS[4][way]:
                 reduce_step(4, way, step)
 
-    def ring_total(piece):
-        total = own_term(piece, 0)
-        for way in range(2):
-            going[piece, way].wait_recv()
-            total = total + recv_buf(piece, way, PARTS[piece][way] - 1)[...].astype(F32)
-        return total
-
-    crossing = []
-    for piece in range(2):
-        xw_out[piece] = ring_total(piece).astype(BF)
-        crossing.append(
-            go(xw_out.at[piece], xw_in.at[piece], sxr.at[piece], rxr.at[piece], partner)
-        )
     kept = [ring_total(2), ring_total(3)]
     wd_out[...] = ring_total(4).astype(BF)
     leave(4, wd_out, wd_out_hbm)
 
-    for copy in back_rows:
+    for copy in back_rows + back_terms:
         copy.wait_recv()
     place = place_ref[...]
     tok_out[...] = lax.dot_general(
-        place, back[:, :, :D].reshape(SLOTS, D), ROWS, preferred_element_type=F32
+        place, back[...].reshape(SLOTS, D), ROWS, preferred_element_type=F32
     ).astype(BF)
     leave(0, tok_out, tok_hbm)
-    terms = back[:, :, D:].reshape(SLOTS, 128)
-    pick = lax.div(lax.broadcasted_iota(jnp.int32, (SLOTS, 128), 0), CAP)
-    pick = pick == lax.broadcasted_iota(jnp.int32, (SLOTS, 128), 1)
-    terms = jnp.where(pick, terms.astype(F32), 0.0).astype(BF)
+    terms = jnp.sum(
+        jnp.where(diagonal[None], jnp.broadcast_to(back_s[...], (N_E, CAP, 128)), 0.0),
+        axis=2, keepdims=True,
+    )
+    pick = (
+        lax.broadcasted_iota(jnp.int32, (N_E, CAP, 128), 0)
+        == lax.broadcasted_iota(jnp.int32, (N_E, CAP, 128), 2)
+    )
+    terms = jnp.where(pick, jnp.broadcast_to(terms, (N_E, CAP, 128)), 0.0)
+    terms = terms.reshape(SLOTS, 128).astype(BF)
     by_expert = lax.dot_general(terms, place, ROWS, preferred_element_type=F32)[:N_E]
     ids = lax.broadcasted_iota(jnp.int32, (N_E, TOK), 0) * EXP_DEV
     line = lax.broadcasted_iota(jnp.int32, (8, TOK), 0)
@@ -448,8 +471,10 @@
         pltpu.VMEM((N_E, CAP, D), BF),
         pltpu.VMEM((N_E, CAP, D), BF),
         pltpu.VMEM((N_E, 1, 128), F32),
-        pltpu.VMEM((N_E, CAP, WIDE), BF),
-        pltpu.VMEM((N_E, CAP, WIDE), BF),
+        pltpu.VMEM((N_E, CAP, D), BF),
+        pltpu.VMEM((N_E, CAP, D), BF),
+        pltpu.VMEM((N_E, 1, 128), F32),
+        pltpu.VMEM((N_E, 1, 128), F32),
         pltpu.VMEM((N_Y, 2, 2, UNIT, 2 * FF), BF),
         pltpu.VMEM((N_Y, 2, 2, DOWN, D), BF),
         pltpu.VMEM((D, 2 * FF), BF),
@@ -472,6 +497,8 @@
         pltpu.VMEM((N_Y, DOWN, D), BF),
         pltpu.VMEM((2, UNIT, FF), BF),
         pltpu.VMEM((2, UNIT, FF), BF),
+        pltpu.VMEM((2, UNIT, FF), BF),
+        pltpu.VMEM((2, UNIT, FF), BF),
         dma((12,)),
         dma((N_E,)), dma((N_E,)), dma((N_E,)), dma((N_E,)),
         dma((N_E,)), dma((N_E,)), dma((N_E,)), dma((N_E,)),
@@ -483,6 +510,8 @@
         dma((5, 2, 4)), dma((5, 2, 4)),
         dma((N_Y,)), dma((N_Y,)),
         dma((2,)), dma((2,)),
+        dma((2,)), dma((2,)),
+        dma((N_E,)), dma((N_E,)),
     ]
     outs = pl.pallas_call(
         kernel,

time: 78.6 us -> 77.8 us (0.990)
  Pallas kernels: 77.8 us -> 77 us
where the time goes in v4:
time: 77.8 us; the launch traced here: 77.7 us
  Pallas kernels  77 us (99%)
    pallas_call x1, Pallas kernels, body(): pl.pallas_call(kernel, out_shape=(shape((TOK, D), BF), shape((8, TOK), BF...  75.3 us
    pallas_call x1, Pallas kernels, body(): pl.pallas_call(hand_over, out_shape=(shape((TOK, D), BF), shape((8, TOK),...  1.77 us

profile of v4, /device:TPU:1, one launch (start us, length us, event | category | flops | bytes accessed | tf_op | source)
XLA Modules:
  0.0 77.7 jit_solution(6705134751916202720)
XLA Ops:
  0.6 75.3 %shard_map.110 = (bf16[128,1280]{1,0:T(8,128)(2,1)}, bf16[8,128]{1,0:T(8,128)(2,1)}, bf16[40,512]{1,0:T(8,128)(2,1)}, bf16[40,512]{1,0:T(8,128)(2,1)}, bf16[16,1280]{1,0:T(8,128)(2,1)}) custom-call(bf16[128,1280]{1,0:T(8,128)(2,1)} %tokens_hbm.1, bf16[128,1280]{1,0:T(8,128)(2,1)} %grads_hbm.1, s32[8,128]{1,0:T(8,128)} %bitcast.3, bf16[8,128]{1,0:T(8,128)(2,1)} %bitcast.4, ...), custom_call_target="tpu_custom_call" | custom-call | tf_op jit(solution)/shard_map/pallas_call | solution.py:516
  75.9 1.8 %shard_map.111 = (bf16[128,1280]{1,0:T(8,128)(2,1)}, bf16[8,128]{1,0:T(8,128)(2,1)}, bf16[1,40,512]{2,1,0:T(8,128)(2,1)}, bf16[1,40,512]{2,1,0:T(8,128)(2,1)}, bf16[1,16,1280]{2,1,0:T(8,128)(2,1)}) custom-call(bf16[128,1280]{1,0:T(8,128)(2,1)} %get-tuple-element.15.refs_0_, bf16[8,128]{1,0:T(8,128)(2,1)} %get-tuple-element.16.refs_1_, ...), custom_call_target="tpu_custom_call" | custom-call | tf_op jit(solution)/shard_map/pallas_call | solution.py:529

commit v5 on v4

--- a/solution.py
+++ b/solution.py
@@ -346,6 +346,12 @@
             srs.at[piece, way, step], rrs.at[piece, way, step], ups[way],
         )
 
+    for offset in (3, -4, 2, -3, 1, -2, -1, 0):
+        index = offset % N_Y
+        xq_out[index] = chip_sum(1, offset, across).astype(BF)
+        swapped[index] = go(
+            xq_out.at[index], xq_in.at[index], sxq.at[index], rxq.at[index], partner
+        )
     far = []
     for piece in range(2):
         lanes = slice(piece * FF, piece * FF + FF)
@@ -353,12 +359,6 @@
         far.append(go(far_out.at[piece], far_in.at[piece], sfr.at[piece], rfr.at[piece], up_two))
         for way in range(2):
             reduce_step(piece, way, 0)
-    for offset in (3, -4, 2, -3, 1, -2, -1, 0):
-        index = offset % N_Y
-        xq_out[index] = chip_sum(1, offset, across).astype(BF)
-        swapped[index] = go(
-            xq_out.at[index], xq_in.at[index], sxq.at[index], rxq.at[index], partner
-        )
     for piece in range(2, 4):
         for way in range(2):
             reduce_step(piece, way, 0)

time: 77.8 us -> 77.5 us (level); the launches traced: 77.7 us -> 76.5 us
  Pallas kernels: 77 us -> 75.8 us
    pallas_call x1, Pallas kernels: 75.3 us -> 74.1 us  [body(): pl.pallas_call(kernel, out_shape=(shape((TOK, D), BF), shape((8, TOK), BF...]
where the time goes in v5:
time: 77.5 us; the launch traced here: 76.5 us
  Pallas kernels  75.8 us (98%)
    pallas_call x1, Pallas kernels, body(): pl.pallas_call(kernel, out_shape=(shape((TOK, D), BF), shape((8, TOK), BF...  74.1 us
    pallas_call x1, Pallas kernels, body(): pl.pallas_call(hand_over, out_shape=(shape((TOK, D), BF), shape((8, TOK),...  1.77 us

profile of v5, /device:TPU:1, one launch (start us, length us, event | category | flops | bytes accessed | tf_op | source)
XLA Modules:
  0.0 76.5 jit_solution(16795911651682015826)
XLA Ops:
  0.6 74.1 %shard_map.110 = (bf16[128,1280]{1,0:T(8,128)(2,1)}, bf16[8,128]{1,0:T(8,128)(2,1)}, bf16[40,512]{1,0:T(8,128)(2,1)}, bf16[40,512]{1,0:T(8,128)(2,1)}, bf16[16,1280]{1,0:T(8,128)(2,1)}) custom-call(bf16[128,1280]{1,0:T(8,128)(2,1)} %tokens_hbm.1, bf16[128,1280]{1,0:T(8,128)(2,1)} %grads_hbm.1, s32[8,128]{1,0:T(8,128)} %bitcast.3, bf16[8,128]{1,0:T(8,128)(2,1)} %bitcast.4, ...), custom_call_target="tpu_custom_call" | custom-call | tf_op jit(solution)/shard_map/pallas_call | solution.py:516
  74.7 1.8 %shard_map.111 = (bf16[128,1280]{1,0:T(8,128)(2,1)}, bf16[8,128]{1,0:T(8,128)(2,1)}, bf16[1,40,512]{2,1,0:T(8,128)(2,1)}, bf16[1,40,512]{2,1,0:T(8,128)(2,1)}, bf16[1,16,1280]{2,1,0:T(8,128)(2,1)}) custom-call(bf16[128,1280]{1,0:T(8,128)(2,1)} %get-tuple-element.15.refs_0_, bf16[8,128]{1,0:T(8,128)(2,1)} %get-tuple-element.16.refs_1_, ...), custom_call_target="tpu_custom_call" | custom-call | tf_op jit(solution)/shard_map/pallas_call | solution.py:529

commit v6 on v5

--- a/solution.py
+++ b/solution.py
@@ -24,7 +24,7 @@
 PEERS = (8, 7, 9, 6, 10, 5, 11, 4, 12, 3, 13, 2, 14, 1, 15)
 STEPS = ((4, 3), (3, 4), (4, 3))
 PARTS = ((3, 3), (3, 3), (3, 4), (3, 4), (3, 4))
-LAST_IN = 3
+LAST_IN = 6
 
 
 def kernel(

time: 77.5 us -> 77 us (level)
  Pallas kernels: 75.8 us -> 75 us
    pallas_call x1, Pallas kernels: 74.1 us -> 73.2 us  [body(): pl.pallas_call(kernel, out_shape=(shape((TOK, D), BF), shape((8, TOK), BF...]
where the time goes in v6:
time: 77 us; the launch traced here: 75.6 us
  Pallas kernels  75 us (97%)
    pallas_call x1, Pallas kernels, body(): pl.pallas_call(kernel, out_shape=(shape((TOK, D), BF), shape((8, TOK), BF...  73.2 us
    pallas_call x1, Pallas kernels, body(): pl.pallas_call(hand_over, out_shape=(shape((TOK, D), BF), shape((8, TOK),...  1.77 us

profile of v6, /device:TPU:1, one launch (start us, length us, event | category | flops | bytes accessed | tf_op | source)
XLA Modules:
  0.0 75.6 jit_solution(5139284852060440347)
XLA Ops:
  0.6 73.2 %shard_map.110 = (bf16[128,1280]{1,0:T(8,128)(2,1)}, bf16[8,128]{1,0:T(8,128)(2,1)}, bf16[40,512]{1,0:T(8,128)(2,1)}, bf16[40,512]{1,0:T(8,128)(2,1)}, bf16[16,1280]{1,0:T(8,128)(2,1)}) custom-call(bf16[128,1280]{1,0:T(8,128)(2,1)} %tokens_hbm.1, bf16[128,1280]{1,0:T(8,128)(2,1)} %grads_hbm.1, s32[8,128]{1,0:T(8,128)} %bitcast.3, bf16[8,128]{1,0:T(8,128)(2,1)} %bitcast.4, ...), custom_call_target="tpu_custom_call" | custom-call | tf_op jit(solution)/shard_map/pallas_call | solution.py:516
  73.9 1.8 %shard_map.111 = (bf16[128,1280]{1,0:T(8,128)(2,1)}, bf16[8,128]{1,0:T(8,128)(2,1)}, bf16[1,40,512]{2,1,0:T(8,128)(2,1)}, bf16[1,40,512]{2,1,0:T(8,128)(2,1)}, bf16[1,16,1280]{2,1,0:T(8,128)(2,1)}) custom-call(bf16[128,1280]{1,0:T(8,128)(2,1)} %get-tuple-element.15.refs_0_, bf16[8,128]{1,0:T(8,128)(2,1)} %get-tuple-element.16.refs_1_, ...), custom_call_target="tpu_custom_call" | custom-call | tf_op jit(solution)/shard_map/pallas_call | solution.py:529
